TPU v7x, 256 devices: a whole 4x4x8 slice. The times are simulated.
256 devices in a mesh: row: 16 (over z, core), col: 16 (over y, x).
Axes of the slice: x: 4, y: 4, z: 8, core: 2. Of those that a mesh axis runs over, the one named last changes fastest.
Arguments:
- iterate: float32 [32768, 256], P(('row', 'col'))
- past_images: float32 [5, 32768, 256], P(None, ('row', 'col'))
- past_residuals: float32 [5, 32768, 256], P(None, ('row', 'col'))
- features: bfloat16 [32768, 128], P(('row', 'col')), may hold values from -6 to 6
- input_weight: bfloat16 [128, 256], replicated, may hold values from -0.5 to 0.5
- mix_weight: bfloat16 [256, 256], replicated, may hold values from -0.375 to 0.375
- tile_values: bfloat16 [16, 16, 256, 128, 128], P('row', 'col'), may hold values from -0.02734375 to 0.02734375
- tile_rows: int32 [16, 16, 256], P('row', 'col'), may hold values from 0 to 15
- tile_cols: int32 [16, 16, 256], P('row', 'col'), may hold values from 0 to 15
- tile_count: int32 [16, 16], P('row', 'col'), may hold values from 1 to 256, as said below
Outputs:
- next_iterate: float32 [32768, 256], P(('row', 'col'))
- last_residual: float32 [32768, 256], P(('row', 'col'))
Inputs may be any that keep to these rules, and one draw needn't show every extreme that they name: `tile_count`: live tile slots of a device; some device has exactly 256.
All inputs are finite; a program needn't handle non-finite values.
Results may differ from a plain program's by a relative error of at most 0.015.
Values may be sent and summed in bfloat16 or wider, within the bound.
A program may use at most 64 MiB of HBM per device.

v0:
```python
import jax
import jax.numpy as jnp
from jax import lax
from jax.sharding import PartitionSpec as P

ITERS = 3


def solve_small(matrix, rhs):
    count = matrix.shape[0]
    lower = {}
    for first in range(count):
        for second in range(first + 1):
            total = matrix[first, second]
            for inner in range(second):
                total = total - lower[first, inner] * lower[second, inner]
            if first == second:
                lower[first, second] = jnp.sqrt(total)
            else:
                lower[first, second] = total / lower[second, second]
    forward = []
    for first in range(count):
        total = rhs[first]
        for inner in range(first):
            total = total - lower[first, inner] * forward[inner]
        forward.append(total / lower[first, first])
    backward = [None] * count
    for first in reversed(range(count)):
        total = forward[first]
        for inner in range(first + 1, count):
            total = total - lower[inner, first] * backward[inner]
        backward[first] = total / lower[first, first]
    return jnp.stack(backward)


def mixing(gram):
    size = gram.shape[0]
    regular = gram + 0.05 * (jnp.trace(gram) / size) * jnp.eye(size, dtype=gram.dtype)
    weights = solve_small(regular, jnp.ones((size,), gram.dtype))
    return weights / jnp.sum(weights)


def local_rows(panel, values, rows_index, cols_index, count, row_tiles):
    tile = values.shape[-1]
    channels = panel.shape[-1]
    panel_tiles = panel.reshape(-1, tile, channels)
    group = 8

    def add_group(group_pos, total):
        first = group_pos * group
        group_values = lax.dynamic_slice_in_dim(values, first, group, 0)
        group_rows = lax.dynamic_slice_in_dim(rows_index, first, group, 0)
        group_cols = lax.dynamic_slice_in_dim(cols_index, first, group, 0)
        live = first + jnp.arange(group, dtype=jnp.int32) < count
        chosen = panel_tiles[group_cols]
        products = jnp.einsum(
            "stu,suh->sth", group_values, chosen, preferred_element_type=jnp.float32
        )
        products = jnp.where(live[:, None, None], products, 0.0)
        return total.at[group_rows].add(products)

    start = jnp.zeros((row_tiles, tile, channels), jnp.float32)
    total = lax.fori_loop(0, (count + group - 1) // group, add_group, start)
    rounded = total.reshape(row_tiles * tile, channels).astype(jnp.bfloat16)
    rounded = lax.optimization_barrier(rounded)
    return rounded.astype(jnp.float32)


def history_gram(residuals):
    return jnp.einsum("aph,bph->ab", residuals, residuals, precision=lax.Precision.HIGHEST)


def on_device(
    iterate,
    past_images,
    past_residuals,
    features,
    input_weight,
    mix_weight,
    tile_values,
    tile_rows,
    tile_cols,
    tile_count,
):
    values = tile_values[0, 0]
    rows_index = tile_rows[0, 0]
    cols_index = tile_cols[0, 0]
    count = tile_count[0, 0]
    owned = iterate.shape[0]
    row_tiles = lax.axis_size("col") * owned // values.shape[-1]
    inject = jnp.dot(features, input_weight, preferred_element_type=jnp.float32)
    state = iterate
    images = past_images
    residuals = past_residuals
    residual = iterate
    for step in range(ITERS):
        lowered = state.astype(jnp.bfloat16)
        message = jnp.dot(lowered, mix_weight, preferred_element_type=jnp.float32).astype(
            jnp.bfloat16
        )
        panel = lax.all_gather(message, "row", axis=0, tiled=True)
        partial_value = local_rows(panel, values, rows_index, cols_index, count, row_tiles)
        summed = lax.psum(partial_value.astype(jnp.bfloat16), "col").astype(jnp.float32)
        aggregate = lax.dynamic_slice_in_dim(summed, lax.axis_index("col") * owned, owned, 0)
        image = jax.nn.relu(aggregate + inject)
        residual = image - state
        images = jnp.concatenate([images[1:], image[None]], axis=0)
        residuals = jnp.concatenate([residuals[1:], residual[None]], axis=0)
        gram = lax.psum(history_gram(residuals), ("row", "col"))
        alpha = mixing(gram)
        state = jnp.sum(alpha[:, None, None] * images, axis=0)
    return (state, residual)


def solution(mesh):
    return jax.shard_map(
        on_device,
        mesh=mesh,
        in_specs=(
            P(("row", "col"), None),
            P(None, ("row", "col"), None),
            P(None, ("row", "col"), None),
            P(("row", "col"), None),
            P(),
            P(),
            P("row", "col", None, None, None),
            P("row", "col", None),
            P("row", "col", None),
            P("row", "col"),
        ),
        out_specs=(P(("row", "col"), None), P(("row", "col"), None)),
        check_vma=False,
    )
```

profile of v0, /device:TPU:1, one launch (start us, length us, event | category | flops | bytes accessed | tf_op | source)
XLA Modules:
  0.0 1258.4 jit_solution(6690753012634895393)
XLA Ops:
  10.5 42.7 %all-gather.4.cloned.1.call-done = bf16[2048,256]{1,0:T(8,128)(2,1)} async-done(((bf16[128,256]{1,0:T(8,128)(2,1)}), bf16[2048,256]{1,0:T(8,128)(2,1)}) %all-gather.4.cloned.1.call-update) | async-done | bytes 1048592 | tf_op jit(solution)/shard_map/all_gather | solution.py:101
  54.8 99.2 %while.30 = (s32[]{:T(128)}, f32[16,128,256]{2,1,0:T(8,128)}, s32[]{:T(128)}, s32[256]{0:T(256)S(1)}, s32[]{:T(128)}, /*index=5*/bf16[256,128,128]{2,1,0:T(8,128...) while((s32[]{:T(128)}, f32[16,128,256]{2,1,0:T(8,128)}, ...), condition=%wide.region_2.3_spmd, body=%wide.region_0.2_spmd.sunk | while | flops 67634248 | bytes 6033827 | solution.py:63
  57.4 3.3 scatter_fusion
  63.3 3.3 scatter_fusion
  69.1 3.3 scatter_fusion
  75.0 3.3 scatter_fusion
  80.9 3.3 scatter_fusion
  86.8 3.2 scatter_fusion
  92.6 3.3 scatter_fusion
  98.4 3.3 scatter_fusion
  104.3 3.3 scatter_fusion
  110.1 3.2 scatter_fusion
  116.0 3.2 scatter_fusion
  121.7 3.2 scatter_fusion
  127.5 3.2 scatter_fusion
  133.3 3.2 scatter_fusion
  139.1 3.3 scatter_fusion
  145.0 3.2 scatter_fusion
  150.7 3.3 scatter_fusion
  157.8 176.8 %all-reduce.4.cloned.1.call-done = bf16[2048,256]{1,0:T(8,128)(2,1)} async-done(((bf16[2048,256]{1,0:T(8,128)(2,1)}), bf16[2048,256]{1,0:T(8,128)(2,1)}) %all-reduce.4.cloned.1.call-update) | async-done | bytes 1048592 | tf_op jit(solution)/shard_map/psum | solution.py:103
  338.1 77.1 %psum.43 = f32[5,5]{1,0:T(8,128)S(1)} all-reduce(f32[5,5]{1,0:T(8,128)S(1)} %convolution_bitcast_fusion.2), channel_id=1, replica_groups=mesh['row'=16,'col'=16] {'row','col'}, use_global_device_ids=true, to_apply=%region_4.5 | all-reduce | flops 25 | bytes 200 | tf_op jit(solution)/shard_map/psum | solution.py:109
  428.5 35.6 %all-gather.6.cloned.1.call-done = bf16[2048,256]{1,0:T(8,128)(2,1)} async-done(((bf16[128,256]{1,0:T(8,128)(2,1)}), bf16[2048,256]{1,0:T(8,128)(2,1)}) %all-gather.6.cloned.1.call-update) | async-done | bytes 1048592 | tf_op jit(solution)/shard_map/all_gather | solution.py:101
  465.7 99.2 %while.31 = (s32[]{:T(128)}, f32[16,128,256]{2,1,0:T(8,128)}, s32[]{:T(128)}, s32[256]{0:T(256)S(1)}, s32[]{:T(128)}, /*index=5*/bf16[256,128,128]{2,1,0:T(8,128...) while((s32[]{:T(128)}, f32[16,128,256]{2,1,0:T(8,128)}, ...), condition=%wide.region_9.10_spmd, body=%wide.region_7.9_spmd.sunk | while | flops 67634248 | bytes 6033827 | solution.py:63
  468.3 3.3 scatter_fusion.1
  474.2 3.3 scatter_fusion.1
  480.0 3.3 scatter_fusion.1
  485.8 3.3 scatter_fusion.1
  491.8 3.3 scatter_fusion.1
  497.7 3.2 scatter_fusion.1
  503.4 3.3 scatter_fusion.1
  509.3 3.3 scatter_fusion.1
  515.1 3.3 scatter_fusion.1
  521.0 3.2 scatter_fusion.1
  526.8 3.2 scatter_fusion.1
  532.6 3.2 scatter_fusion.1
  538.4 3.2 scatter_fusion.1
  544.2 3.2 scatter_fusion.1
  550.0 3.3 scatter_fusion.1
  555.8 3.2 scatter_fusion.1
  561.6 3.3 scatter_fusion.1
  567.7 177.8 %all-reduce.6.cloned.1.call-done = bf16[2048,256]{1,0:T(8,128)(2,1)} async-done(((bf16[2048,256]{1,0:T(8,128)(2,1)}), bf16[2048,256]{1,0:T(8,128)(2,1)}) %all-reduce.6.cloned.1.call-update) | async-done | bytes 1048592 | tf_op jit(solution)/shard_map/psum | solution.py:103
  749.8 77.1 %psum.45 = f32[5,5]{1,0:T(8,128)S(1)} all-reduce(f32[5,5]{1,0:T(8,128)S(1)} %convolution_bitcast_fusion.1), channel_id=1, replica_groups=mesh['row'=16,'col'=16] {'row','col'}, use_global_device_ids=true, to_apply=%region_11.12 | all-reduce | flops 25 | bytes 200 | tf_op jit(solution)/shard_map/psum | solution.py:109
  840.7 35.6 %all-gather.8.cloned.1.call-done = bf16[2048,256]{1,0:T(8,128)(2,1)} async-done(((bf16[128,256]{1,0:T(8,128)(2,1)}), bf16[2048,256]{1,0:T(8,128)(2,1)}) %all-gather.8.cloned.1.call-update) | async-done | bytes 1048592 | tf_op jit(solution)/shard_map/all_gather | solution.py:101
  877.8 99.2 %while.32 = (s32[]{:T(128)}, f32[16,128,256]{2,1,0:T(8,128)}, s32[]{:T(128)}, s32[256]{0:T(256)S(1)}, s32[]{:T(128)}, /*index=5*/bf16[256,128,128]{2,1,0:T(8,128...) while((s32[]{:T(128)}, f32[16,128,256]{2,1,0:T(8,128)}, ...), condition=%wide.region_16.17_spmd, body=%wide.region_14.16_spmd.sunk | while | flops 67634248 | bytes 6033827 | solution.py:63
  880.4 3.3 scatter_fusion.2
  886.3 3.3 scatter_fusion.2
  892.1 3.3 scatter_fusion.2
  898.0 3.3 scatter_fusion.2
  903.9 3.3 scatter_fusion.2
  909.8 3.2 scatter_fusion.2
  915.6 3.3 scatter_fusion.2
  921.4 3.3 scatter_fusion.2
  927.3 3.3 scatter_fusion.2
  933.1 3.2 scatter_fusion.2
  938.9 3.2 scatter_fusion.2
  944.7 3.2 scatter_fusion.2
  950.5 3.2 scatter_fusion.2
  956.3 3.2 scatter_fusion.2
  962.1 3.3 scatter_fusion.2
  968.0 3.2 scatter_fusion.2
  973.7 3.3 scatter_fusion.2
  977.0 2.8 convert_element_type.66
  979.8 177.8 %all-reduce.8.cloned.1.call-done = bf16[2048,256]{1,0:T(8,128)(2,1)} async-done(((bf16[2048,256]{1,0:T(8,128)(2,1)}), bf16[2048,256]{1,0:T(8,128)(2,1)}) %all-reduce.8.cloned.1.call-update) | async-done | bytes 1048592 | tf_op jit(solution)/shard_map/psum | solution.py:103
  1161.3 77.1 %psum.47 = f32[5,5]{1,0:T(8,128)S(1)} all-reduce(f32[5,5]{1,0:T(8,128)S(1)} %convolution_bitcast_fusion), channel_id=1, replica_groups=mesh['row'=16,'col'=16] {'row','col'}, use_global_device_ids=true, to_apply=%region_18.19 | all-reduce | flops 25 | bytes 200 | tf_op jit(solution)/shard_map/psum | solution.py:109
  (357 shorter events, 162.9 us)
Async XLA Ops:
  7.2 0.9 copy-start
  7.2 47.6 %copy-start.21 = (s32[1,1,256]{2,1,0:T(1,128)S(1)}, s32[1,1,256]{2,1,0:T(1,128)}, u32[]{:S(2)}) copy-start(s32[1,1,256]{2,1,0:T(1,128)} %param.23) | copy-start | bytes 3076
  7.2 47.6 %copy-start.22 = (s32[1,1,256]{2,1,0:T(1,128)S(1)}, s32[1,1,256]{2,1,0:T(1,128)}, u32[]{:S(2)}) copy-start(s32[1,1,256]{2,1,0:T(1,128)} %param.24) | copy-start | bytes 3076
  7.2 46.1 %all-gather.4.cloned.1.call-start = ((), (), s32[]{:S(2)}) async-start(), calls=%async_computation | async-start | bytes 1114112 | tf_op jit(solution)/shard_map/all_gather | solution.py:101
  9.8 324.8 %all-reduce.4.cloned.1.call-start = ((), (), s32[]{:S(2)}) async-start(), calls=%async_computation.1 | async-start | bytes 2097152 | tf_op jit(solution)/shard_map/psum | solution.py:103
  53.3 1.6 copy-start.1
  154.0 2.9 slice-start
  156.8 0.8 copy-start.20
  156.8 0.8 copy-start.23
  156.8 177.8 %copy-start.13 = (f32[128,256]{1,0:T(8,128)S(1)}, f32[128,256]{1,0:T(8,128)}, u32[]{:S(2)}) copy-start(f32[128,256]{1,0:T(8,128)} %param.16) | copy-start | bytes 393220
  156.8 181.2 %copy-start.15 = (f32[5,128,256]{2,1,0:T(8,128)S(1)}, f32[5,128,256]{2,1,0:T(8,128)}, u32[]{:S(2)}) copy-start(f32[5,128,256]{2,1,0:T(8,128)} %param.17) | copy-start | bytes 1966084
  156.8 307.3 %all-gather.6.cloned.1.call-start = ((), (), s32[]{:S(2)}) async-start(), calls=%async_computation.2 | async-start | bytes 1114112 | tf_op jit(solution)/shard_map/all_gather | solution.py:101
  157.1 270.5 %copy-start.10 = (f32[4,128,256]{1,0,2:T(4,128)}, f32[4,128,256]{1,0,2:T(4,128)S(1)}, u32[]{:S(2)}) copy-start(f32[4,128,256]{1,0,2:T(4,128)S(1)} %copy.16) | copy-start | bytes 1572868
  335.4 130.2 %copy-start.6 = (f32[1,128,256]{2,1,0:T(8,128)}, f32[1,128,256]{2,1,0:T(8,128)S(1)}, u32[]{:S(2)}) copy-start(f32[1,128,256]{2,1,0:T(8,128)S(1)} %get-tuple-element.193) | copy-start | bytes 393220
  335.5 410.9 %copy-start.16 = (f32[1,128,256]{1,0,2:T(1,128)}, f32[1,128,256]{1,0,2:T(1,128)S(1)}, u32[]{:S(2)}) copy-start(f32[1,128,256]{1,0,2:T(1,128)S(1)} %copy.13) | copy-start | bytes 393220
  338.1 127.6 %copy-start.4 = (f32[4,128,256]{2,1,0:T(8,128)}, f32[4,128,256]{2,1,0:T(8,128)S(1)}, u32[]{:S(2)}) copy-start(f32[4,128,256]{2,1,0:T(8,128)S(1)} %slice.170) | copy-start | bytes 1572868
  428.5 317.0 %all-reduce.6.cloned.1.call-start = ((), (), s32[]{:S(2)}) async-start(), calls=%async_computation.3 | async-start | bytes 2097152 | tf_op jit(solution)/shard_map/psum | solution.py:103
  464.1 1.6 copy-start.3
  564.9 182.2 %copy-start.11 = (f32[4,128,256]{1,0,2:T(4,128)S(1)}, f32[4,128,256]{1,0,2:T(4,128)}, u32[]{:S(2)}) copy-start(f32[4,128,256]{1,0,2:T(4,128)} %copy-done.10) | copy-start | bytes 1572868
  567.6 182.1 %copy-start.5 = (f32[4,128,256]{2,1,0:T(8,128)S(1)}, f32[4,128,256]{2,1,0:T(8,128)}, u32[]{:S(2)}) copy-start(f32[4,128,256]{2,1,0:T(8,128)} %copy-done.4) | copy-start | bytes 1572868
  567.6 182.1 %copy-start.7 = (f32[1,128,256]{2,1,0:T(8,128)S(1)}, f32[1,128,256]{2,1,0:T(8,128)}, u32[]{:S(2)}) copy-start(f32[1,128,256]{2,1,0:T(8,128)} %copy-done.6) | copy-start | bytes 393220
  567.7 308.6 %all-gather.8.cloned.1.call-start = ((), (), s32[]{:S(2)}) async-start(), calls=%async_computation.4 | async-start | bytes 1114112 | tf_op jit(solution)/shard_map/all_gather | solution.py:101
  746.5 0.7 copy-start.18
  839.2 0.7 copy-start.8
  840.6 317.0 %all-reduce.8.cloned.1.call-start = ((), (), s32[]{:S(2)}) async-start(), calls=%async_computation.5 | async-start | bytes 2097152 | tf_op jit(solution)/shard_map/psum | solution.py:103
  876.3 1.6 copy-start.2
  977.0 180.7 %copy-start.9 = (f32[128,256]{1,0:T(8,128)S(1)}, f32[128,256]{1,0:T(8,128)}, u32[]{:S(2)}) copy-start(f32[128,256]{1,0:T(8,128)} %copy-done.8) | copy-start | bytes 393220
  977.0 181.6 %copy-start.12 = (f32[4,128,256]{1,0,2:T(4,128)S(1)}, f32[4,128,256]{1,0,2:T(4,128)}, u32[]{:S(2)}) copy-start(f32[4,128,256]{1,0,2:T(4,128)} %copy-done.10) | copy-start | bytes 1572868
  977.0 181.6 %copy-start.17 = (f32[1,128,256]{1,0,2:T(1,128)S(1)}, f32[1,128,256]{1,0,2:T(1,128)}, u32[]{:S(2)}) copy-start(f32[1,128,256]{1,0,2:T(1,128)} %copy-done.16) | copy-start | bytes 393220
  977.0 181.7 %copy-start.19 = (f32[1,128,256]{1,0,2:T(1,128)S(1)}, f32[1,128,256]{1,0,2:T(1,128)}, u32[]{:S(2)}) copy-start(f32[1,128,256]{1,0,2:T(1,128)} %copy-done.18) | copy-start | bytes 393220
  1158.5 93.0 %copy-start.14 = (f32[128,256]{1,0:T(8,128)}, f32[128,256]{1,0:T(8,128)S(1)}, u32[]{:S(2)}) copy-start(f32[128,256]{1,0:T(8,128)S(1)} %get-tuple-element.188) | copy-start | bytes 393220
Sparse Core Ops, SparseCore 0:
  10.4 42.7 all-gather.3
  156.9 177.5 all-reduce.3
  428.6 35.4 all-gather.5
  567.8 177.6 all-reduce.5
  840.8 35.4 all-gather.7
  980.0 177.6 all-reduce.7
where the time goes:
time: 1270 us; the launch traced here: 1260 us
  waiting for transfers between devices  646 us (51%)
  blocking collectives  231 us (18%)
  other arithmetic  218 us (17%)
  matrix products  74.2 us (6%)
  between operations  47.8 us (4%)
  local copies, waits for them, and re-layouts  39.8 us (3%)
    psum x3, waiting for transfers between devices, on_device(): lax.psum(partial_value.astype(jnp.bfloat16), 'col').astype(jnp.float32)  532 us
    psum x3, blocking collectives, on_device(): gram = lax.psum(history_gram(residuals), ('row', 'col'))  231 us
    scatter-add x51, other arithmetic, add_group(): return total.at[group_rows].add(products)  166 us
    all_gather x3, waiting for transfers between devices, on_device(): panel = lax.all_gather(message, 'row', axis=0, tiled=True)  114 us
    dot_general x51, matrix products, add_group(): jnp.einsum('stu,suh->sth', group_values, chosen, preferred_element_type=j...  63.1 us
    lt x51, other arithmetic, add_group(): live = first + jnp.arange(group, dtype=jnp.int32) < count  33.3 us
    gather x51, local copies, waits for them, and re-layouts, add_group(): chosen = panel_tiles[group_cols]  29.6 us
  transfers between devices with their start and end apart: 6, of which 6 were waited for; matrix products, arithmetic and copies ran while one was open for 0% of the time, Pallas kernels for 0%

commit v1 on v0

v1 whole, which is shorter than its diff:
```python
import jax
import jax.numpy as jnp
from jax import lax
from jax.experimental import pallas as pl
from jax.experimental.pallas import tpu as pltpu
from jax.sharding import PartitionSpec as P

ITERS = 3
TILE = 128
HALF = 64
CHANNELS = 256
MESH = pl.DeviceIdType.MESH
F32 = jnp.float32
BF16 = jnp.bfloat16
CHUNKS = 8
SLOTS = 256


def build_kernel(rows_ref, cols_ref, count_ref, values_ref, dense_ref, buf, acc, out, in_sem, out_sem):
    size = SLOTS // CHUNKS
    loads = []
    for chunk in range(CHUNKS):
        span = pl.ds(chunk * size, size)
        loads.append(pltpu.make_async_copy(values_ref.at[span], buf.at[span], in_sem.at[chunk]))
        loads[-1].start()
    count = count_ref[0]

    @pl.loop(0, 256)
    def _(cell):
        acc[cell] = jnp.zeros((TILE, TILE), F32)

    for chunk in range(CHUNKS):
        loads[chunk].wait()

        @pl.loop(chunk * size, jnp.minimum(count, (chunk + 1) * size))
        def _(slot):
            cell = cols_ref[slot] * 16 + rows_ref[slot]
            acc[cell] += buf[slot].astype(F32)

    stores = []
    for col_tile in range(16):

        @pl.loop(0, 16)
        def _(row_tile):
            out[col_tile, row_tile] = acc[col_tile * 16 + row_tile].astype(BF16)

        stores.append(pltpu.make_async_copy(out.at[col_tile], dense_ref.at[col_tile], out_sem.at[col_tile]))
        stores[-1].start()
    for store in stores:
        store.wait()


def build_dense(rows, cols, count, values):
    return pl.pallas_call(
        build_kernel,
        out_shape=jax.ShapeDtypeStruct((16, 16, TILE, TILE), BF16),
        in_specs=[pl.BlockSpec(memory_space=pltpu.SMEM)] * 3 + [pl.BlockSpec(memory_space=pl.ANY)],
        out_specs=pl.BlockSpec(memory_space=pl.ANY),
        scratch_shapes=[
            pltpu.VMEM((SLOTS, TILE, TILE), BF16),
            pltpu.VMEM((256, TILE, TILE), F32),
            pltpu.VMEM((16, 16, TILE, TILE), BF16),
            pltpu.SemaphoreType.DMA((CHUNKS,)),
            pltpu.SemaphoreType.DMA((16,)),
        ],
        compiler_params=pltpu.CompilerParams(vmem_limit_bytes=44 * 1024 * 1024),
        name="build_dense",
    )(rows, cols, count, values)


def mixing_weights(gram):
    trace = gram[0, 0]
    for pos in range(1, 5):
        trace = trace + gram[pos, pos]
    shift = 0.05 * (trace / 5.0)
    lower = {}
    for first in range(5):
        for second in range(first + 1):
            total = gram[first, second]
            if first == second:
                total = total + shift
            for inner in range(second):
                total = total - lower[first, inner] * lower[second, inner]
            if first == second:
                lower[first, second] = jnp.sqrt(total)
            else:
                lower[first, second] = total / lower[second, second]
    forward = []
    for first in range(5):
        total = jnp.ones_like(trace)
        for inner in range(first):
            total = total - lower[first, inner] * forward[inner]
        forward.append(total / lower[first, first])
    backward = [None] * 5
    for first in reversed(range(5)):
        total = forward[first]
        for inner in range(first + 1, 5):
            total = total - lower[inner, first] * backward[inner]
        backward[first] = total / lower[first, first]
    norm = backward[0]
    for pos in range(1, 5):
        norm = norm + backward[pos]
    return [value / norm for value in backward]


OLD_PAIRS = [(first, second) for first in range(4) for second in range(first + 1)]


def lane_sums(left, right):
    return jnp.sum(left[:, :TILE] * right[:, :TILE] + left[:, TILE:] * right[:, TILE:], axis=0, keepdims=True)


def main_kernel(
    iterate_ref, features_ref, input_weight_ref, mix_weight_ref, past_images_ref, past_residuals_ref, dense_ref,
    state_out, residual_out,
    dense, panel, acc, part_a, part_b, got_a1, got_b1, sum_a, sum_b, got_a2, got_b2,
    state, inject, images, residuals, pack, gram_send1, gram_send2, gram_got1, gram_got2,
    load_sem, ag_send, ag_recv, a1_send, a1_recv, b1_send, b1_recv, a2_send, a2_recv, b2_send, b2_recv,
    g1_send, g1_recv, g2_send, g2_recv,
):
    row = lax.axis_index("row")
    col = lax.axis_index("col")
    z, core = row // 2, lax.rem(row, 2)
    y, x = col // 4, lax.rem(col, 4)
    sibling = row + 1 - 2 * core

    load_dense = pltpu.make_async_copy(dense_ref, dense, load_sem.at[0])
    load_images = pltpu.make_async_copy(past_images_ref.at[pl.ds(1, 4)], images.at[pl.ds(0, 4)], load_sem.at[1])
    load_residuals = pltpu.make_async_copy(
        past_residuals_ref.at[pl.ds(1, 4)], residuals.at[pl.ds(0, 4)], load_sem.at[2]
    )
    load_dense.start()
    load_images.start()
    load_residuals.start()

    barrier = pltpu.get_barrier_semaphore()

    @pl.loop(1, 16)
    def _(step):
        pl.semaphore_signal(barrier, inc=1, device_id=(row, lax.rem(col + step, 16)), device_id_type=MESH)
        pl.semaphore_signal(barrier, inc=1, device_id=(lax.rem(row + step, 16), col), device_id_type=MESH)

    state[...] = iterate_ref[...]
    inject[...] = jnp.dot(features_ref[...], input_weight_ref[...], preferred_element_type=F32)
    pack[...] = jnp.zeros_like(pack)
    pl.semaphore_wait(barrier, 30)

    def chip(offset):
        return lax.rem(z + offset + 8, 8)

    @pl.loop(0, ITERS)
    def _(k):
        panel[row] = jnp.dot(state[...].astype(BF16), mix_weight_ref[...], preferred_element_type=F32).astype(BF16)
        sends = []

        def send(src, dst, sem, target):
            copy = pltpu.make_async_remote_copy(
                src_ref=src,
                dst_ref=dst,
                send_sem=ag_send.at[len(sends)],
                recv_sem=sem,
                device_id=(target, col),
                device_id_type=MESH,
            )
            copy.start()
            sends.append(copy)

        def block(tile):
            return panel.at[tile]

        def arrive(tile, ref=None, sem=None):
            ref = block(tile) if ref is None else ref
            sem = ag_recv.at[tile] if sem is None else sem
            pltpu.make_async_copy(ref, ref, sem).wait()

        up, down = 2 * chip(1) + core, 2 * chip(-1) + core
        send(block(row), block(row), ag_recv.at[row], up)
        send(block(row), block(row), ag_recv.at[row], down)
        send(block(row), block(row), ag_recv.at[row], sibling)

        def multiply(pos, first=False, last=False):
            rhs = panel[pl.ds(2 * pos, 2)].reshape(2 * TILE, CHANNELS)

            @pl.loop(0, 4)
            def _(group):
                rows = pl.ds(4 * group, 4)
                left = dense[2 * pos, rows].reshape(4 * TILE, TILE)
                right = dense[2 * pos + 1, rows].reshape(4 * TILE, TILE)
                product = jnp.dot(jnp.concatenate([left, right], axis=1), rhs, preferred_element_type=F32)
                if first:
                    acc[group] = product
                elif not last:
                    acc[group] += product
                else:
                    total = (acc[group] + product).astype(BF16)
                    for tile in range(4):
                        part_a[tile, group] = total[tile * TILE : tile * TILE + HALF]
                        part_b[group, tile] = total[tile * TILE + HALF : (tile + 1) * TILE]

        @pl.when(k == 0)
        def _():
            load_images.wait()
            load_residuals.wait()

        for pos, (first, second) in enumerate(OLD_PAIRS):
            pack[5 + pos : 6 + pos, :] = lane_sums(residuals[k + first], residuals[k + second])

        @pl.when(k == 0)
        def _():
            load_dense.wait()

        low, high = pl.ds(0, HALF), pl.ds(HALF, HALF)
        far = 2 * chip(4) + core
        for step in range(1, 4):
            for sign in (-1, 1):
                tile = 2 * chip(sign * step) + core
                target = up if sign < 0 else down
                arrive(tile)
                if step < 3:
                    send(block(tile), block(tile), ag_recv.at[tile], target)
                else:
                    part = low if sign < 0 else high
                    sem = ag_recv.at[tile] if sign < 0 else ag_recv.at[16]
                    send(panel.at[tile, part], panel.at[tile, part], sem, target)
                send(block(tile), block(tile), ag_recv.at[tile], sibling)
            if step == 1:
                arrive(sibling)
                multiply(z, first=True)
            else:
                for sign in (-1, 1):
                    arrive(2 * chip(sign * (step - 1)) + 1 - core)
                    multiply(chip(sign * (step - 1)))
        for sign in (-1, 1):
            arrive(2 * chip(sign * 3) + 1 - core)
            multiply(chip(sign * 3))
        arrive(far, panel.at[far, low])
        arrive(far, panel.at[far, high], ag_recv.at[16])
        send(block(far), block(far), ag_recv.at[far], sibling)
        arrive(2 * chip(4) + 1 - core)
        multiply(chip(4), last=True)

        copies = []
        for step in range(1, 4):
            to_x, to_y = lax.rem(x + step, 4), lax.rem(y + step, 4)
            copies.append(pltpu.make_async_remote_copy(
                src_ref=part_a.at[to_x], dst_ref=got_a1.at[x], send_sem=a1_send.at[step], recv_sem=a1_recv.at[x],
                device_id=(row, 4 * y + to_x), device_id_type=MESH,
            ))
            copies.append(pltpu.make_async_remote_copy(
                src_ref=part_b.at[to_y], dst_ref=got_b1.at[y], send_sem=b1_send.at[step], recv_sem=b1_recv.at[y],
                device_id=(row, 4 * to_y + x), device_id_type=MESH,
            ))
        for copy in copies:
            copy.start()
        for copy in sends:
            copy.wait_send()
        for step in range(1, 4):
            from_x, from_y = lax.rem(x + 4 - step, 4), lax.rem(y + 4 - step, 4)
            pltpu.make_async_copy(got_a1.at[from_x], got_a1.at[from_x], a1_recv.at[from_x]).wait()
            pltpu.make_async_copy(got_b1.at[from_y], got_b1.at[from_y], b1_recv.at[from_y]).wait()
        for step in range(1, 5):
            to_x, to_y = lax.rem(x + step, 4), lax.rem(y + step, 4)
            total_a = part_a[x, to_y].astype(F32)
            total_b = part_b[y, to_x].astype(F32)
            for other in range(1, 4):
                total_a += got_a1[lax.rem(x + other, 4), to_y].astype(F32)
                total_b += got_b1[lax.rem(y + other, 4), to_x].astype(F32)
            sum_a[to_y] = total_a.astype(BF16)
            sum_b[to_x] = total_b.astype(BF16)
            if step == 4:
                break
            copy_a = pltpu.make_async_remote_copy(
                src_ref=sum_a.at[to_y], dst_ref=got_a2.at[y], send_sem=a2_send.at[step], recv_sem=a2_recv.at[y],
                device_id=(row, 4 * to_y + x), device_id_type=MESH,
            )
            copy_b = pltpu.make_async_remote_copy(
                src_ref=sum_b.at[to_x], dst_ref=got_b2.at[x], send_sem=b2_send.at[step], recv_sem=b2_recv.at[x],
                device_id=(row, 4 * y + to_x), device_id_type=MESH,
            )
            copy_a.start()
            copy_b.start()
            copies += [copy_a, copy_b]
        for step in range(1, 4):
            from_x, from_y = lax.rem(x + 4 - step, 4), lax.rem(y + 4 - step, 4)
            pltpu.make_async_copy(got_a2.at[from_y], got_a2.at[from_y], a2_recv.at[from_y]).wait()
            pltpu.make_async_copy(got_b2.at[from_x], got_b2.at[from_x], b2_recv.at[from_x]).wait()
        total_a = sum_a[y].astype(F32)
        total_b = sum_b[x].astype(F32)
        for other in range(1, 4):
            total_a += got_a2[lax.rem(y + other, 4)].astype(F32)
            total_b += got_b2[lax.rem(x + other, 4)].astype(F32)
        image_a = jnp.maximum(total_a + inject[:HALF], 0.0)
        image_b = jnp.maximum(total_b + inject[HALF:], 0.0)
        images[k + 4, pl.ds(0, HALF)] = image_a
        images[k + 4, pl.ds(HALF, HALF)] = image_b
        residuals[k + 4, pl.ds(0, HALF)] = image_a - state[:HALF]
        residuals[k + 4, pl.ds(HALF, HALF)] = image_b - state[HALF:]
        for copy in copies:
            copy.wait_send()

        residual = residuals[k + 4]
        for pos in range(5):
            pack[pos : pos + 1, :] = lane_sums(residual, residuals[k + pos])
        head, tail = pack[0:8], pack[8:16]
        lanes = lax.broadcasted_iota(jnp.int32, (8, TILE), 1)
        own = jnp.where(lanes < 64, head + pltpu.roll(head, 64, 1), tail + pltpu.roll(tail, 64, 1))
        gram_send1[...] = own
        gram_got1[col] = own

        def gram1(step):
            to = lax.rem(col + step, 16)
            return pltpu.make_async_remote_copy(
                src_ref=gram_send1, dst_ref=gram_got1.at[col], send_sem=g1_send.at[step], recv_sem=g1_recv.at[col],
                device_id=(row, to), device_id_type=MESH,
            )

        def gram2(step):
            to = lax.rem(row + step, 16)
            return pltpu.make_async_remote_copy(
                src_ref=gram_send2, dst_ref=gram_got2.at[row], send_sem=g2_send.at[step], recv_sem=g2_recv.at[row],
                device_id=(to, col), device_id_type=MESH,
            )

        @pl.loop(1, 16)
        def _(step):
            gram1(step).start()

        @pl.loop(1, 16)
        def _(step):
            source = lax.rem(col + step, 16)
            pltpu.make_async_copy(gram_got1.at[source], gram_got1.at[source], g1_recv.at[source]).wait()

        own = jnp.sum(gram_got1[...], axis=0)
        gram_send2[...] = own
        gram_got2[row] = own

        @pl.loop(1, 16)
        def _(step):
            gram2(step).start()

        @pl.loop(1, 16)
        def _(step):
            source = lax.rem(row + step, 16)
            pltpu.make_async_copy(gram_got2.at[source], gram_got2.at[source], g2_recv.at[source]).wait()

        whole = jnp.sum(gram_got2[...], axis=0)
        head = jnp.sum(jnp.where(lanes < 64, whole, 0.0), axis=1, keepdims=True)
        tail = jnp.sum(jnp.where(lanes < 64, 0.0, whole), axis=1, keepdims=True)
        head = jnp.broadcast_to(head, (8, TILE))
        tail = jnp.broadcast_to(tail, (8, TILE))
        values = [head[pos : pos + 1] for pos in range(8)] + [tail[pos : pos + 1] for pos in range(8)]
        gram = {(4, pos): values[pos] for pos in range(5)}
        for pos, pair in enumerate(OLD_PAIRS):
            gram[pair] = values[5 + pos]
        alpha = mixing_weights(gram)
        alpha = [jnp.concatenate([value, value], axis=1) for value in alpha]
        mixed = alpha[0] * images[k]
        for pos in range(1, 5):
            mixed += alpha[pos] * images[k + pos]
        state[...] = mixed

        @pl.loop(1, 16)
        def _(step):
            gram1(step).wait_send()
            gram2(step).wait_send()

    state_out[...] = state[...]
    residual_out[...] = residuals[ITERS + 3]


def on_device(
    iterate,
    past_images,
    past_residuals,
    features,
    input_weight,
    mix_weight,
    tile_values,
    tile_rows,
    tile_cols,
    tile_count,
):
    dense = build_dense(tile_rows[0, 0], tile_cols[0, 0], tile_count[0], tile_values[0, 0])
    dma = pltpu.SemaphoreType.DMA
    vmem = pl.BlockSpec(memory_space=pltpu.VMEM)
    hbm = pl.BlockSpec(memory_space=pl.ANY)
    block = jax.ShapeDtypeStruct((TILE, CHANNELS), F32)
    quad = pltpu.VMEM((4, 4, HALF, CHANNELS), BF16)
    single = pltpu.VMEM((4, HALF, CHANNELS), BF16)
    return pl.pallas_call(
        main_kernel,
        out_shape=(block, block),
        in_specs=[vmem] * 4 + [hbm] * 3,
        out_specs=(vmem, vmem),
        scratch_shapes=[
            pltpu.VMEM((16, 16, TILE, TILE), BF16),
            pltpu.VMEM((16, TILE, CHANNELS), BF16),
            pltpu.VMEM((4, 4 * TILE, CHANNELS), F32),
            quad, quad, quad, quad, single, single, single, single,
            pltpu.VMEM((TILE, CHANNELS), F32),
            pltpu.VMEM((TILE, CHANNELS), F32),
            pltpu.VMEM((ITERS + 4, TILE, CHANNELS), F32),
            pltpu.VMEM((ITERS + 4, TILE, CHANNELS), F32),
            pltpu.VMEM((16, TILE), F32),
            pltpu.VMEM((8, TILE), F32),
            pltpu.VMEM((8, TILE), F32),
            pltpu.VMEM((16, 8, TILE), F32),
            pltpu.VMEM((16, 8, TILE), F32),
            dma((3,)), dma((16,)), dma((17,)),
            dma((4,)), dma((4,)), dma((4,)), dma((4,)), dma((4,)), dma((4,)), dma((4,)), dma((4,)),
            dma((16,)), dma((16,)), dma((16,)), dma((16,)),
        ],
        compiler_params=pltpu.CompilerParams(
            collective_id=0, has_side_effects=True, vmem_limit_bytes=40 * 1024 * 1024
        ),
        name="anderson",
    )(iterate, features, input_weight, mix_weight, past_images, past_residuals, dense)


def solution(mesh):
    return jax.shard_map(
        on_device,
        mesh=mesh,
        in_specs=(
            P(("row", "col"), None),
            P(None, ("row", "col"), None),
            P(None, ("row", "col"), None),
            P(("row", "col"), None),
            P(),
            P(),
            P("row", "col", None, None, None),
            P("row", "col", None),
            P("row", "col", None),
            P("row", "col"),
        ),
        out_specs=(P(("row", "col"), None), P(("row", "col"), None)),
        check_vma=False,
    )
```

time: 1270 us -> 141 us (0.11)
  waiting for transfers between devices: 646 us -> 0 us
  blocking collectives: 231 us -> 0 us
  other arithmetic: 218 us -> 0 us
  Pallas kernels: 0 us -> 137 us
  matrix products: 74.2 us -> 0 us
  between operations: 47.8 us -> 1.37 us
  local copies, waits for them, and re-layouts: 39.8 us -> 2.69 us
    psum x3 -> x0, waiting for transfers between devices: 532 us -> none  [on_device(): lax.psum(partial_value.astype(jnp.bfloat16), 'col').astype(jnp.float32)]
    psum x3 -> x0, blocking collectives: 231 us -> none  [on_device(): gram = lax.psum(history_gram(residuals), ('row', 'col'))]
    scatter-add x51 -> x0, other arithmetic: 166 us -> none  [add_group(): return total.at[group_rows].add(products)]
    pallas_call x0 -> x2, Pallas kernels: none -> 137 us  [the longest x1 131 us: on_device(): pl.pallas_call(main_kernel, out_shape=(block, block), in_specs=[vmem] * 4...]
    all_gather x3 -> x0, waiting for transfers between devices: 114 us -> none  [on_device(): panel = lax.all_gather(message, 'row', axis=0, tiled=True)]
    dot_general x58 -> x0, matrix products: 74.2 us -> none  [the longest x51 63.1 us: add_group(): jnp.einsum('stu,suh->sth', group_values, chosen, preferred_element_type=j...]
    lt x51 -> x0, other arithmetic: 33.3 us -> none  [add_group(): live = first + jnp.arange(group, dtype=jnp.int32) < count]
    gather x51 -> x0, local copies, waits for them, and re-layouts: 29.6 us -> none  [add_group(): chosen = panel_tiles[group_cols]]
  transfers between devices with their start and end apart: 6 -> 0, of which waited for: 6 -> 0; matrix products, arithmetic and copies ran while one was open for 0% -> 0% of each run, Pallas kernels for 0% -> 0%
where the time goes in v1:
time: 141 us
  Pallas kernels  137 us (97%)
  local copies, waits for them, and re-layouts  2.69 us (2%)
    pallas_call x1, Pallas kernels, on_device(): pl.pallas_call(main_kernel, out_shape=(block, block), in_specs=[vmem] * 4...  131 us
    pallas_call x1, Pallas kernels, build_dense(): pl.pallas_call(build_kernel, out_shape=jax.ShapeDtypeStruct((16, 16, TILE...  6.61 us

profile of v1, /device:TPU:1, one launch (start us, length us, event | category | flops | bytes accessed | tf_op | source)
XLA Modules:
  0.0 141.2 jit_solution(7716973456622267768)
XLA Ops:
  1.3 0.0 copy-start.6
  1.3 0.7 copy-done.6
  2.0 0.0 copy-start.7
  2.0 0.7 copy-done.7
  2.6 0.0 copy-start
  2.6 0.0 copy-start.1
  2.6 0.0 copy-start.2
  2.6 0.0 copy-start.3
  2.7 0.0 copy-start.4
  2.7 0.0 copy-start.5
  2.7 6.6 %build_dense.1.dense_ref = bf16[16,16,128,128]{3,2,1,0:T(8,128)(2,1)S(1)} custom-call(s32[256]{0:T(256)S(1)} %bitcast.5, s32[256]{0:T(256)S(1)} %bitcast.6, s32[1]{0:T(128)} %bitcast.4.count_ref, bf16[256,128,128]{2,1,0:T(8,128)(2,1)} %bitcast.7), custom_call_target="tpu_custom_call" | custom-call | tf_op jit(solution)/shard_map/build_dense/pallas_call | solution.py:54
  9.3 0.0 copy-done
  9.3 0.0 copy-done.1
  9.3 0.0 copy-done.2
  9.3 0.0 copy-done.3
  9.3 0.0 copy-done.4
  9.3 0.0 copy-done.5
  9.3 130.6 %anderson.1 = (f32[128,256]{1,0:T(8,128)S(1)}, f32[128,256]{1,0:T(8,128)S(1)}) custom-call(f32[128,256]{1,0:T(8,128)S(1)} %copy-done.2, bf16[128,128]{1,0:T(8,128)(2,1)S(1)} %copy-done.5, bf16[128,256]{1,0:T(8,128)(2,1)S(1)} %copy-done.4, bf16[256,256]{1,0:T(8,128)(2,1)S(1)} %copy-done.3, f32[5,128,256]{2,1,0:T(8,128)S(1)} %copy-done, ...), custom_call_target="tpu_custom_call" | custom-call | tf_op jit(solution)/shard_map/anderson/pallas_call | solution.py:390
  139.9 0.7 copy.15
  140.6 0.7 copy.16
Async XLA Ops:
  1.3 0.7 copy-start.6
  2.0 0.7 copy-start.7
  2.6 6.7 %copy-start = (f32[5,128,256]{2,1,0:T(8,128)S(1)}, f32[5,128,256]{2,1,0:T(8,128)}, u32[]{:S(2)}) copy-start(f32[5,128,256]{2,1,0:T(8,128)} %past_images_ref.1) | copy-start | bytes 1966084
  2.6 6.7 %copy-start.1 = (f32[5,128,256]{2,1,0:T(8,128)S(1)}, f32[5,128,256]{2,1,0:T(8,128)}, u32[]{:S(2)}) copy-start(f32[5,128,256]{2,1,0:T(8,128)} %past_residuals_ref.1) | copy-start | bytes 1966084
  2.6 6.7 %copy-start.2 = (f32[128,256]{1,0:T(8,128)S(1)}, f32[128,256]{1,0:T(8,128)}, u32[]{:S(2)}) copy-start(f32[128,256]{1,0:T(8,128)} %iterate_ref.1) | copy-start | bytes 393220
  2.6 6.7 %copy-start.3 = (bf16[256,256]{1,0:T(8,128)(2,1)S(1)}, bf16[256,256]{1,0:T(8,128)(2,1)}, u32[]{:S(2)}) copy-start(bf16[256,256]{1,0:T(8,128)(2,1)} %mix_weight_ref.1) | copy-start | bytes 393220
  2.7 6.7 %copy-start.4 = (bf16[128,256]{1,0:T(8,128)(2,1)S(1)}, bf16[128,256]{1,0:T(8,128)(2,1)}, u32[]{:S(2)}) copy-start(bf16[128,256]{1,0:T(8,128)(2,1)} %input_weight_ref.1) | copy-start | bytes 196612
  2.7 6.7 %copy-start.5 = (bf16[128,128]{1,0:T(8,128)(2,1)S(1)}, bf16[128,128]{1,0:T(8,128)(2,1)}, u32[]{:S(2)}) copy-start(bf16[128,128]{1,0:T(8,128)(2,1)} %features_ref.1) | copy-start | bytes 98308

commit v2 on v0

v2 whole, which is shorter than its diff:
```python
import jax
import jax.numpy as jnp
from jax import lax
from jax.experimental import pallas as pl
from jax.experimental.pallas import tpu as pltpu
from jax.sharding import PartitionSpec as P

ITERS = 3
TILE = 128
HALF = 64
CHANNELS = 256
MESH = pl.DeviceIdType.MESH
F32 = jnp.float32
BF16 = jnp.bfloat16
CHUNKS = 8
SLOTS = 256


def build_kernel(rows_hbm, cols_hbm, count_ref, values_ref, dense_ref, rows_ref, cols_ref, buf, acc, in_sem, index_sem):
    size = SLOTS // CHUNKS
    index_loads = [
        pltpu.make_async_copy(rows_hbm.at[0, 0], rows_ref, index_sem.at[0]),
        pltpu.make_async_copy(cols_hbm.at[0, 0], cols_ref, index_sem.at[1]),
    ]
    for load in index_loads:
        load.start()
    loads = []
    for chunk in range(CHUNKS):
        span = pl.ds(chunk * size, size)
        loads.append(pltpu.make_async_copy(values_ref.at[span], buf.at[span], in_sem.at[chunk]))
        loads[-1].start()
    count = count_ref[0]

    @pl.loop(0, 256, unroll=8)
    def _(cell):
        acc[cell] = jnp.zeros((TILE, TILE), F32)

    for load in index_loads:
        load.wait()
    for chunk in range(CHUNKS):
        loads[chunk].wait()

        @pl.loop(chunk * size, jnp.minimum(count, (chunk + 1) * size))
        def _(slot):
            cell = cols_ref[slot] * 16 + rows_ref[slot]
            acc[cell] += buf[slot].astype(F32)

    @pl.loop(0, 256, unroll=8)
    def _(cell):
        dense_ref[cell] = acc[cell].astype(BF16)


def build_dense(rows, cols, count, values):
    hbm = pl.BlockSpec(memory_space=pltpu.HBM)
    return pl.pallas_call(
        build_kernel,
        out_shape=jax.ShapeDtypeStruct((256, TILE, TILE), BF16),
        in_specs=[hbm, hbm, pl.BlockSpec(memory_space=pltpu.SMEM), hbm],
        out_specs=pl.BlockSpec(memory_space=pltpu.VMEM),
        scratch_shapes=[
            pltpu.SMEM((SLOTS,), jnp.int32),
            pltpu.SMEM((SLOTS,), jnp.int32),
            pltpu.VMEM((SLOTS, TILE, TILE), BF16),
            pltpu.VMEM((256, TILE, TILE), F32),
            pltpu.SemaphoreType.DMA((CHUNKS,)),
            pltpu.SemaphoreType.DMA((2,)),
        ],
        compiler_params=pltpu.CompilerParams(vmem_limit_bytes=40 * 1024 * 1024),
        name="build_dense",
    )(rows, cols, count, values)


def mixing_weights(gram):
    trace = gram[0, 0]
    for pos in range(1, 5):
        trace = trace + gram[pos, pos]
    shift = 0.05 * (trace / 5.0)
    lower = {}
    for first in range(5):
        for second in range(first + 1):
            total = gram[first, second]
            if first == second:
                total = total + shift
            for inner in range(second):
                total = total - lower[first, inner] * lower[second, inner]
            if first == second:
                lower[first, second] = jnp.sqrt(total)
            else:
                lower[first, second] = total / lower[second, second]
    forward = []
    for first in range(5):
        total = jnp.ones_like(trace)
        for inner in range(first):
            total = total - lower[first, inner] * forward[inner]
        forward.append(total / lower[first, first])
    backward = [None] * 5
    for first in reversed(range(5)):
        total = forward[first]
        for inner in range(first + 1, 5):
            total = total - lower[inner, first] * backward[inner]
        backward[first] = total / lower[first, first]
    norm = backward[0]
    for pos in range(1, 5):
        norm = norm + backward[pos]
    return [value / norm for value in backward]


OLD_PAIRS = [(first, second) for first in range(4) for second in range(first + 1)]


def lane_sums(left, right):
    return jnp.sum(left * right, axis=0, keepdims=True)


def main_kernel(
    iterate_ref, features_ref, input_weight_ref, mix_weight_ref, past_images_ref, past_residuals_ref, dense,
    state_out, residual_out,
    panel, acc, part, got1, sums, got2,
    state, inject, images, residuals, pack, gram_send1, gram_send2, gram_got1, gram_got2,
    load_sem, ag_send, ag_recv, rs1_send, rs1_recv, rs2_send, rs2_recv, gram_sem,
):
    row = lax.axis_index("row")
    col = lax.axis_index("col")
    z, core = row // 2, lax.rem(row, 2)
    y, x = col // 4, lax.rem(col, 4)
    first_axis, second_axis = (x, y), (y, x)
    sibling = row + 1 - 2 * core

    loads = []
    for half in range(2):
        for past_ref, kept in ((past_images_ref, images), (past_residuals_ref, residuals)):
            source = past_ref.at[pl.ds(1, 4), :, pl.ds(half * TILE, TILE)]
            loads.append(pltpu.make_async_copy(source, kept.at[pl.ds(0, 4), half], load_sem.at[len(loads)]))
            loads[-1].start()

    barrier = pltpu.get_barrier_semaphore()

    @pl.loop(1, 16)
    def _(step):
        pl.semaphore_signal(barrier, inc=1, device_id=(row, lax.rem(col + step, 16)), device_id_type=MESH)
        pl.semaphore_signal(barrier, inc=1, device_id=(lax.rem(row + step, 16), col), device_id_type=MESH)

    state[...] = iterate_ref[...]
    inject[...] = jnp.dot(features_ref[...], input_weight_ref[...], preferred_element_type=F32)
    pack[...] = jnp.zeros_like(pack)
    pl.semaphore_wait(barrier, 30)

    def chip(offset):
        return lax.rem(z + offset + 8, 8)

    def own_tile(offset):
        return 2 * chip(offset) + core

    def twin_tile(offset):
        return 2 * chip(offset) + 1 - core

    def gather_send(half, ref, target, slot, recv):
        return pltpu.make_async_remote_copy(
            src_ref=ref,
            dst_ref=ref,
            send_sem=ag_send.at[half, slot],
            recv_sem=ag_recv.at[half, recv],
            device_id=(target, col),
            device_id_type=MESH,
        )

    def gather_wait(half, tile, part=None, recv=None):
        ref = panel.at[half, tile] if part is None else panel.at[half, tile, part]
        pltpu.make_async_copy(ref, ref, ag_recv.at[half, tile if recv is None else recv]).wait()

    def multiply(half, spots, first=False, last=False):
        rhs = jnp.concatenate([panel[half, 2 * spot + side] for spot in spots for side in range(2)], axis=0)
        lhs = [dense[pl.ds(16 * (2 * spot + side), 16)].reshape(16 * TILE, TILE) for spot in spots for side in range(2)]
        product = jnp.dot(jnp.concatenate(lhs, axis=1), rhs, preferred_element_type=F32)
        if first:
            acc[half] = product
        elif not last:
            acc[half] += product
        else:
            total = (acc[half] + product).astype(BF16)
            for tile in range(16):
                tile_y, tile_x = tile // 4, tile % 4
                part[half, 0, tile_x, tile_y] = total[tile * TILE : tile * TILE + HALF]
                part[half, 1, tile_y, tile_x] = total[tile * TILE + HALF : (tile + 1) * TILE]

    def all_waits(ref, sem):
        pltpu.make_async_copy(ref, ref, sem).wait()

    def scatter1(half, way, step):
        to = lax.rem(first_axis[way] + step, 4)
        return pltpu.make_async_remote_copy(
            src_ref=part.at[half, way, to], dst_ref=got1.at[half, way, first_axis[way]],
            send_sem=rs1_send.at[half, way], recv_sem=rs1_recv.at[half, way],
            device_id=(row, 4 * y + to if way == 0 else 4 * to + x), device_id_type=MESH,
        )

    def scatter2(half, way, step):
        to = lax.rem(second_axis[way] + step, 4)
        return pltpu.make_async_remote_copy(
            src_ref=sums.at[half, way, to], dst_ref=got2.at[half, way, second_axis[way]],
            send_sem=rs2_send.at[half, way], recv_sem=rs2_recv.at[half, way],
            device_id=(row, 4 * to + x if way == 0 else 4 * y + to), device_id_type=MESH,
        )

    def gram1(step):
        to = lax.rem(col + step, 16)
        return pltpu.make_async_remote_copy(
            src_ref=gram_send1, dst_ref=gram_got1.at[col], send_sem=gram_sem.at[0], recv_sem=gram_sem.at[1],
            device_id=(row, to), device_id_type=MESH,
        )

    def gram2(step):
        to = lax.rem(row + step, 16)
        return pltpu.make_async_remote_copy(
            src_ref=gram_send2, dst_ref=gram_got2.at[row], send_sem=gram_sem.at[2], recv_sem=gram_sem.at[3],
            device_id=(to, col), device_id_type=MESH,
        )

    @pl.loop(0, ITERS)
    def _(k):
        message = jnp.dot(state[...].astype(BF16), mix_weight_ref[...], preferred_element_type=F32).astype(BF16)
        sends = []
        used = [0, 0]

        def send(half, tile, target, part=None, recv=None):
            ref = panel.at[half, tile] if part is None else panel.at[half, tile, part]
            sends.append(gather_send(half, ref, target, used[half], tile if recv is None else recv))
            sends[-1].start()
            used[half] += 1

        for half in range(2):
            panel[half, row] = message[:, half * TILE : (half + 1) * TILE]
            for offset in (2, -2, 0, 1, -1):
                send(half, row, sibling if offset == 0 else own_tile(offset))

        @pl.when(k == 0)
        def _():
            for load in loads:
                load.wait()

        for pos, (first, second) in enumerate(OLD_PAIRS):
            pack[5 + pos : 6 + pos, :] = sum(lane_sums(residuals[k + first, half], residuals[k + second, half]) for half in range(2))

        low, high = pl.ds(0, TILE // 2), pl.ds(TILE // 2, TILE // 2)

        def near(half):
            for sign, part, extra in ((-1, low, None), (1, high, 16)):
                tile = own_tile(2 * sign)
                gather_wait(half, tile)
                send(half, tile, own_tile(-2 * sign), part, tile if extra is None else extra)
                send(half, tile, own_tile(-sign))
                send(half, tile, sibling)
            for sign in (-1, 1):
                gather_wait(half, own_tile(sign))
                send(half, own_tile(sign), sibling)

        def product(half, *offsets, **where):
            for offset in offsets:
                gather_wait(half, twin_tile(offset))
            multiply(half, [chip(offset) for offset in offsets], **where)

        def distant(half):
            for offset in (-3, 3):
                gather_wait(half, own_tile(offset))
                send(half, own_tile(offset), sibling)
            gather_wait(half, own_tile(4), low)
            gather_wait(half, own_tile(4), high, 16)
            send(half, own_tile(4), sibling)

        def scatter(half):
            for step in (2, 1, 3):
                for way in range(2):
                    scatter1(half, way, step).start()

        near(0)
        product(0, 0, first=True)
        near(1)
        product(0, 1, -1)
        product(0, 2, -2)
        product(1, 0, first=True)
        distant(0)
        product(1, 1, -1)
        product(0, 3, -3)
        product(0, 4, last=True)
        scatter(0)
        distant(1)
        product(1, 2, -2)
        product(1, 3, -3)
        product(1, 4, last=True)
        scatter(1)

        for half in range(2):
            for way in range(2):
                all_waits(got1.at[half, way, pl.ds(0, 3)], rs1_recv.at[half, way])
                total = part[half, way, first_axis[way]].astype(F32)
                for step in range(1, 4):
                    total += got1[half, way, lax.rem(first_axis[way] + step, 4)].astype(F32)
                sums[half, way] = total.astype(BF16)
                for step in (2, 1, 3):
                    scatter2(half, way, step).start()

        scores = [0.0] * 5
        for half in range(2):
            lanes = slice(half * TILE, (half + 1) * TILE)
            for way in range(2):
                rows = slice(way * HALF, (way + 1) * HALF)
                all_waits(got2.at[half, way, pl.ds(0, 3)], rs2_recv.at[half, way])
                total = sums[half, way, second_axis[way]].astype(F32)
                for step in range(1, 4):
                    total += got2[half, way, lax.rem(second_axis[way] + step, 4)].astype(F32)
                image = jnp.maximum(total + inject[rows, lanes], 0.0)
                residual = image - state[rows, lanes]
                images[k + 4, half, rows] = image
                residuals[k + 4, half, rows] = residual
                for pos in range(5):
                    other = residual if pos == 4 else residuals[k + pos, half, rows]
                    scores[pos] = scores[pos] + lane_sums(residual, other)

        for pos in range(5):
            pack[pos : pos + 1, :] = scores[pos]
        head, tail = pack[0:8], pack[8:16]
        lanes = lax.broadcasted_iota(jnp.int32, (8, TILE), 1)
        own = jnp.where(lanes < 64, head + pltpu.roll(head, 64, 1), tail + pltpu.roll(tail, 64, 1))
        gram_send1[...] = own
        gram_got1[col] = own

        @pl.loop(1, 16, unroll=5)
        def _(step):
            gram1(step).start()

        for copy in sends:
            copy.wait_send()

        for half in range(2):
            for way in range(2):
                all_waits(part.at[half, way, pl.ds(0, 3)], rs1_send.at[half, way])
                all_waits(sums.at[half, way, pl.ds(0, 3)], rs2_send.at[half, way])
        all_waits(gram_got1.at[pl.ds(0, 15)], gram_sem.at[1])

        own = jnp.sum(gram_got1[...], axis=0)
        gram_send2[...] = own
        gram_got2[row] = own

        @pl.loop(1, 16, unroll=5)
        def _(step):
            gram2(step).start()

        all_waits(gram_got2.at[pl.ds(0, 15)], gram_sem.at[3])

        whole = jnp.sum(gram_got2[...], axis=0)
        head = jnp.sum(jnp.where(lanes < 64, whole, 0.0), axis=1, keepdims=True)
        tail = jnp.sum(jnp.where(lanes < 64, 0.0, whole), axis=1, keepdims=True)
        head = jnp.broadcast_to(head, (8, TILE))
        tail = jnp.broadcast_to(tail, (8, TILE))
        values = [head[pos : pos + 1] for pos in range(8)] + [tail[pos : pos + 1] for pos in range(8)]
        gram = {(4, pos): values[pos] for pos in range(5)}
        for pos, pair in enumerate(OLD_PAIRS):
            gram[pair] = values[5 + pos]
        alpha = mixing_weights(gram)
        for half in range(2):
            mixed = alpha[0] * images[k, half]
            for pos in range(1, 5):
                mixed += alpha[pos] * images[k + pos, half]
            state[:, half * TILE : (half + 1) * TILE] = mixed

        all_waits(gram_got1.at[pl.ds(0, 15)], gram_sem.at[0])
        all_waits(gram_got2.at[pl.ds(0, 15)], gram_sem.at[2])

    state_out[...] = state[...]
    for half in range(2):
        residual_out[:, half * TILE : (half + 1) * TILE] = residuals[ITERS + 3, half]


def on_device(
    iterate,
    past_images,
    past_residuals,
    features,
    input_weight,
    mix_weight,
    tile_values,
    tile_rows,
    tile_cols,
    tile_count,
):
    dense = build_dense(tile_rows, tile_cols, tile_count[0], tile_values[0, 0])
    dma = pltpu.SemaphoreType.DMA
    vmem = pl.BlockSpec(memory_space=pltpu.VMEM)
    hbm = pl.BlockSpec(memory_space=pl.ANY)
    block = jax.ShapeDtypeStruct((TILE, CHANNELS), F32)
    history = pltpu.VMEM((ITERS + 4, 2, TILE, TILE), F32)
    quads = pltpu.VMEM((2, 2, 4, 4, HALF, TILE), BF16)
    singles = pltpu.VMEM((2, 2, 4, HALF, TILE), BF16)
    return pl.pallas_call(
        main_kernel,
        out_shape=(block, block),
        in_specs=[vmem] * 4 + [hbm] * 2 + [vmem],
        out_specs=(vmem, vmem),
        scratch_shapes=[
            pltpu.VMEM((2, 16, TILE, TILE), BF16),
            pltpu.VMEM((2, 16 * TILE, TILE), F32),
            quads, quads, singles, singles,
            pltpu.VMEM((TILE, CHANNELS), F32),
            pltpu.VMEM((TILE, CHANNELS), F32),
            history,
            history,
            pltpu.VMEM((16, TILE), F32),
            pltpu.VMEM((8, TILE), F32),
            pltpu.VMEM((8, TILE), F32),
            pltpu.VMEM((16, 8, TILE), F32),
            pltpu.VMEM((16, 8, TILE), F32),
            dma((4,)), dma((2, 16)), dma((2, 17)), dma((2, 2)), dma((2, 2)), dma((2, 2)), dma((2, 2)), dma((4,)),
        ],
        compiler_params=pltpu.CompilerParams(
            collective_id=0, has_side_effects=True, vmem_limit_bytes=24 * 1024 * 1024
        ),
        name="anderson",
    )(iterate, features, input_weight, mix_weight, past_images, past_residuals, dense)


def solution(mesh):
    return jax.shard_map(
        on_device,
        mesh=mesh,
        in_specs=(
            P(("row", "col"), None),
            P(None, ("row", "col"), None),
            P(None, ("row", "col"), None),
            P(("row", "col"), None),
            P(),
            P(),
            P("row", "col", None, None, None),
            P("row", "col", None),
            P("row", "col", None),
            P("row", "col"),
        ),
        out_specs=(P(("row", "col"), None), P(("row", "col"), None)),
        check_vma=False,
    )
```

time: 1270 us -> 129 us (0.10)
  waiting for transfers between devices: 646 us -> 0 us
  blocking collectives: 231 us -> 0 us
  other arithmetic: 218 us -> 0 us
  Pallas kernels: 0 us -> 124 us
  matrix products: 74.2 us -> 0 us
  between operations: 47.8 us -> 1.37 us
  local copies, waits for them, and re-layouts: 39.8 us -> 2.69 us
    psum x3 -> x0, waiting for transfers between devices: 532 us -> none  [on_device(): lax.psum(partial_value.astype(jnp.bfloat16), 'col').astype(jnp.float32)]
    psum x3 -> x0, blocking collectives: 231 us -> none  [on_device(): gram = lax.psum(history_gram(residuals), ('row', 'col'))]
    scatter-add x51 -> x0, other arithmetic: 166 us -> none  [add_group(): return total.at[group_rows].add(products)]
    pallas_call x0 -> x2, Pallas kernels: none -> 124 us  [the longest x1 120 us: on_device(): pl.pallas_call(main_kernel, out_shape=(block, block), in_specs=[vmem] * 4...]
    all_gather x3 -> x0, waiting for transfers between devices: 114 us -> none  [on_device(): panel = lax.all_gather(message, 'row', axis=0, tiled=True)]
    dot_general x58 -> x0, matrix products: 74.2 us -> none  [the longest x51 63.1 us: add_group(): jnp.einsum('stu,suh->sth', group_values, chosen, preferred_element_type=j...]
    lt x51 -> x0, other arithmetic: 33.3 us -> none  [add_group(): live = first + jnp.arange(group, dtype=jnp.int32) < count]
    gather x51 -> x0, local copies, waits for them, and re-layouts: 29.6 us -> none  [add_group(): chosen = panel_tiles[group_cols]]
  transfers between devices with their start and end apart: 6 -> 0, of which waited for: 6 -> 0; matrix products, arithmetic and copies ran while one was open for 0% -> 0% of each run, Pallas kernels for 0% -> 0%
where the time goes in v2:
time: 129 us; the launch traced here: 128 us
  Pallas kernels  124 us (96%)
  local copies, waits for them, and re-layouts  2.69 us (2%)
  between operations  1.37 us (1%)
    pallas_call x1, Pallas kernels, on_device(): pl.pallas_call(main_kernel, out_shape=(block, block), in_specs=[vmem] * 4...  120 us
    pallas_call x1, Pallas kernels, build_dense(): pl.pallas_call(build_kernel, out_shape=jax.ShapeDtypeStruct((256, TILE, T...  4.52 us
    unnamed x18, local copies, waits for them, and re-layouts  2.69 us

profile of v2, /device:TPU:1, one launch (start us, length us, event | category | flops | bytes accessed | tf_op | source)
XLA Modules:
  0.0 128.5 jit_solution(6429107196276790886)
XLA Ops:
  1.3 0.0 copy-start.6
  1.3 0.7 copy-done.6
  2.0 0.0 copy-start.7
  2.0 0.7 copy-done.7
  2.6 0.0 copy-start
  2.6 0.0 copy-start.1
  2.6 0.0 copy-start.2
  2.6 0.0 copy-start.3
  2.7 0.0 copy-start.4
  2.7 0.0 copy-start.5
  2.7 4.5 %build_dense.1.dense = bf16[256,128,128]{2,1,0:T(8,128)(2,1)S(1)} custom-call(s32[1,1,256]{2,1,0:T(1,128)S(1)} %copy-done.6, s32[1,1,256]{2,1,0:T(1,128)S(1)} %copy-done.7, s32[1]{0:T(128)} %bitcast.2.count_ref, bf16[256,128,128]{2,1,0:T(8,128)(2,1)} %bitcast.3), custom_call_target="tpu_custom_call" | custom-call | tf_op jit(solution)/shard_map/build_dense/pallas_call | solution.py:55
  7.2 0.0 copy-done
  7.2 0.0 copy-done.1
  7.2 0.0 copy-done.2
  7.2 0.0 copy-done.3
  7.2 0.0 copy-done.4
  7.3 0.0 copy-done.5
  7.3 119.9 %anderson.1 = (f32[128,256]{1,0:T(8,128)S(1)}, f32[128,256]{1,0:T(8,128)S(1)}) custom-call(f32[128,256]{1,0:T(8,128)S(1)} %copy-done.2, bf16[128,128]{1,0:T(8,128)(2,1)S(1)} %copy-done.5, bf16[128,256]{1,0:T(8,128)(2,1)S(1)} %copy-done.4, bf16[256,256]{1,0:T(8,128)(2,1)S(1)} %copy-done.3, f32[5,128,256]{2,1,0:T(8,128)S(1)} %copy-done, ...), custom_call_target="tpu_custom_call" | custom-call | tf_op jit(solution)/shard_map/anderson/pallas_call | solution.py:394
  127.2 0.7 copy.15
  127.8 0.7 copy.16
Async XLA Ops:
  1.3 0.7 copy-start.6
  2.0 0.7 copy-start.7
  2.6 4.6 %copy-start = (f32[5,128,256]{2,1,0:T(8,128)S(1)}, f32[5,128,256]{2,1,0:T(8,128)}, u32[]{:S(2)}) copy-start(f32[5,128,256]{2,1,0:T(8,128)} %past_images_ref.1) | copy-start | bytes 1966084
  2.6 4.6 %copy-start.1 = (f32[5,128,256]{2,1,0:T(8,128)S(1)}, f32[5,128,256]{2,1,0:T(8,128)}, u32[]{:S(2)}) copy-start(f32[5,128,256]{2,1,0:T(8,128)} %past_residuals_ref.1) | copy-start | bytes 1966084
  2.6 4.6 %copy-start.2 = (f32[128,256]{1,0:T(8,128)S(1)}, f32[128,256]{1,0:T(8,128)}, u32[]{:S(2)}) copy-start(f32[128,256]{1,0:T(8,128)} %iterate_ref.1) | copy-start | bytes 393220
  2.6 4.6 %copy-start.3 = (bf16[256,256]{1,0:T(8,128)(2,1)S(1)}, bf16[256,256]{1,0:T(8,128)(2,1)}, u32[]{:S(2)}) copy-start(bf16[256,256]{1,0:T(8,128)(2,1)} %mix_weight_ref.1) | copy-start | bytes 393220
  2.7 4.6 %copy-start.4 = (bf16[128,256]{1,0:T(8,128)(2,1)S(1)}, bf16[128,256]{1,0:T(8,128)(2,1)}, u32[]{:S(2)}) copy-start(bf16[128,256]{1,0:T(8,128)(2,1)} %input_weight_ref.1) | copy-start | bytes 196612
  2.7 4.6 %copy-start.5 = (bf16[128,128]{1,0:T(8,128)(2,1)S(1)}, bf16[128,128]{1,0:T(8,128)(2,1)}, u32[]{:S(2)}) copy-start(bf16[128,128]{1,0:T(8,128)(2,1)} %features_ref.1) | copy-start | bytes 98308

commit v3 on v2

--- a/solution.py
+++ b/solution.py
@@ -16,14 +16,8 @@
 SLOTS = 256
 
 
-def build_kernel(rows_hbm, cols_hbm, count_ref, values_ref, dense_ref, rows_ref, cols_ref, buf, acc, in_sem, index_sem):
+def build_kernel(cells_ref, count_ref, values_ref, dense_ref, buf, acc, in_sem):
     size = SLOTS // CHUNKS
-    index_loads = [
-        pltpu.make_async_copy(rows_hbm.at[0, 0], rows_ref, index_sem.at[0]),
-        pltpu.make_async_copy(cols_hbm.at[0, 0], cols_ref, index_sem.at[1]),
-    ]
-    for load in index_loads:
-        load.start()
     loads = []
     for chunk in range(CHUNKS):
         span = pl.ds(chunk * size, size)
@@ -35,39 +29,33 @@
     def _(cell):
         acc[cell] = jnp.zeros((TILE, TILE), F32)
 
-    for load in index_loads:
-        load.wait()
     for chunk in range(CHUNKS):
         loads[chunk].wait()
 
         @pl.loop(chunk * size, jnp.minimum(count, (chunk + 1) * size))
         def _(slot):
-            cell = cols_ref[slot] * 16 + rows_ref[slot]
-            acc[cell] += buf[slot].astype(F32)
+            acc[cells_ref[slot]] += buf[slot].astype(F32)
 
     @pl.loop(0, 256, unroll=8)
     def _(cell):
         dense_ref[cell] = acc[cell].astype(BF16)
 
 
-def build_dense(rows, cols, count, values):
-    hbm = pl.BlockSpec(memory_space=pltpu.HBM)
+def build_dense(cells, count, values):
+    smem = pl.BlockSpec(memory_space=pltpu.SMEM)
     return pl.pallas_call(
         build_kernel,
         out_shape=jax.ShapeDtypeStruct((256, TILE, TILE), BF16),
-        in_specs=[hbm, hbm, pl.BlockSpec(memory_space=pltpu.SMEM), hbm],
+        in_specs=[smem, smem, pl.BlockSpec(memory_space=pl.ANY)],
         out_specs=pl.BlockSpec(memory_space=pltpu.VMEM),
         scratch_shapes=[
-            pltpu.SMEM((SLOTS,), jnp.int32),
-            pltpu.SMEM((SLOTS,), jnp.int32),
             pltpu.VMEM((SLOTS, TILE, TILE), BF16),
             pltpu.VMEM((256, TILE, TILE), F32),
             pltpu.SemaphoreType.DMA((CHUNKS,)),
-            pltpu.SemaphoreType.DMA((2,)),
         ],
         compiler_params=pltpu.CompilerParams(vmem_limit_bytes=40 * 1024 * 1024),
         name="build_dense",
-    )(rows, cols, count, values)
+    )(cells, count, values)
 
 
 def mixing_weights(gram):
@@ -75,37 +63,42 @@
     for pos in range(1, 5):
         trace = trace + gram[pos, pos]
     shift = 0.05 * (trace / 5.0)
-    lower = {}
-    for first in range(5):
-        for second in range(first + 1):
-            total = gram[first, second]
-            if first == second:
-                total = total + shift
-            for inner in range(second):
-                total = total - lower[first, inner] * lower[second, inner]
-            if first == second:
-                lower[first, second] = jnp.sqrt(total)
-            else:
-                lower[first, second] = total / lower[second, second]
-    forward = []
-    for first in range(5):
-        total = jnp.ones_like(trace)
-        for inner in range(first):
-            total = total - lower[first, inner] * forward[inner]
-        forward.append(total / lower[first, first])
-    backward = [None] * 5
+    left = dict(gram)
+    for pos in range(5):
+        left[pos, pos] = left[pos, pos] + shift
+    right = [jnp.ones_like(trace)] * 5
+    inverse = []
+    for pivot in range(5):
+        inverse.append(1.0 / left[pivot, pivot])
+        for first in range(pivot + 1, 5):
+            factor = left[first, pivot] * inverse[pivot]
+            for second in range(pivot + 1, first + 1):
+                left[first, second] = left[first, second] - factor * left[second, pivot]
+            right[first] = right[first] - factor * right[pivot]
+    weights = [None] * 5
     for first in reversed(range(5)):
-        total = forward[first]
+        total = right[first]
         for inner in range(first + 1, 5):
-            total = total - lower[inner, first] * backward[inner]
-        backward[first] = total / lower[first, first]
-    norm = backward[0]
+            total = total - left[inner, first] * weights[inner]
+        weights[first] = total * inverse[first]
+    norm = weights[0]
     for pos in range(1, 5):
-        norm = norm + backward[pos]
-    return [value / norm for value in backward]
+        norm = norm + weights[pos]
+    scale = 1.0 / norm
+    return [value * scale for value in weights]
 
 
 OLD_PAIRS = [(first, second) for first in range(4) for second in range(first + 1)]
+
+
+FAR_COL = sorted(
+    [(over_y, over_x) for over_y in range(4) for over_x in range(4)][1:],
+    key=lambda over: -sum(min(step, 4 - step) for step in over),
+)
+FAR_ROW = sorted(
+    [(over_z, over_core) for over_z in range(8) for over_core in range(2)][1:],
+    key=lambda over: -min(over[0], 8 - over[0]),
+)
 
 
 def lane_sums(left, right):
@@ -168,20 +161,25 @@
         ref = panel.at[half, tile] if part is None else panel.at[half, tile, part]
         pltpu.make_async_copy(ref, ref, ag_recv.at[half, tile if recv is None else recv]).wait()
 
-    def multiply(half, spots, first=False, last=False):
-        rhs = jnp.concatenate([panel[half, 2 * spot + side] for spot in spots for side in range(2)], axis=0)
-        lhs = [dense[pl.ds(16 * (2 * spot + side), 16)].reshape(16 * TILE, TILE) for spot in spots for side in range(2)]
-        product = jnp.dot(jnp.concatenate(lhs, axis=1), rhs, preferred_element_type=F32)
-        if first:
-            acc[half] = product
-        elif not last:
-            acc[half] += product
-        else:
-            total = (acc[half] + product).astype(BF16)
-            for tile in range(16):
-                tile_y, tile_x = tile // 4, tile % 4
-                part[half, 0, tile_x, tile_y] = total[tile * TILE : tile * TILE + HALF]
-                part[half, 1, tile_y, tile_x] = total[tile * TILE + HALF : (tile + 1) * TILE]
+    def multiply(halves, spots, first=False, last=False):
+        tiles = [2 * spot + side for spot in spots for side in range(2)]
+        rhs = jnp.concatenate(
+            [jnp.concatenate([panel[half, tile] for tile in tiles], axis=0) for half in halves], axis=1
+        )
+        lhs = jnp.concatenate([dense[pl.ds(16 * tile, 16)].reshape(16 * TILE, TILE) for tile in tiles], axis=1)
+        product = jnp.dot(lhs, rhs, preferred_element_type=F32)
+        for pos, half in enumerate(halves):
+            term = product[:, pos * TILE : (pos + 1) * TILE]
+            if first:
+                acc[half] = term
+            elif not last:
+                acc[half] += term
+            else:
+                total = (acc[half] + term).astype(BF16)
+                for tile in range(16):
+                    tile_y, tile_x = tile // 4, tile % 4
+                    part[half, 0, tile_x, tile_y] = total[tile * TILE : tile * TILE + HALF]
+                    part[half, 1, tile_y, tile_x] = total[tile * TILE + HALF : (tile + 1) * TILE]
 
     def all_waits(ref, sem):
         pltpu.make_async_copy(ref, ref, sem).wait()
@@ -202,15 +200,15 @@
             device_id=(row, 4 * to + x if way == 0 else 4 * y + to), device_id_type=MESH,
         )
 
-    def gram1(step):
-        to = lax.rem(col + step, 16)
+    def gram1(over_y, over_x):
+        to = 4 * lax.rem(y + over_y, 4) + lax.rem(x + over_x, 4)
         return pltpu.make_async_remote_copy(
             src_ref=gram_send1, dst_ref=gram_got1.at[col], send_sem=gram_sem.at[0], recv_sem=gram_sem.at[1],
             device_id=(row, to), device_id_type=MESH,
         )
 
-    def gram2(step):
-        to = lax.rem(row + step, 16)
+    def gram2(over_z, over_core):
+        to = 2 * lax.rem(z + over_z, 8) + lax.rem(core + over_core, 2)
         return pltpu.make_async_remote_copy(
             src_ref=gram_send2, dst_ref=gram_got2.at[row], send_sem=gram_sem.at[2], recv_sem=gram_sem.at[3],
             device_id=(to, col), device_id_type=MESH,
@@ -254,10 +252,11 @@
                 gather_wait(half, own_tile(sign))
                 send(half, own_tile(sign), sibling)
 
-        def product(half, *offsets, **where):
-            for offset in offsets:
-                gather_wait(half, twin_tile(offset))
-            multiply(half, [chip(offset) for offset in offsets], **where)
+        def product(halves, *offsets, **where):
+            for half in halves:
+                for offset in offsets:
+                    gather_wait(half, twin_tile(offset))
+            multiply(halves, [chip(offset) for offset in offsets], **where)
 
         def distant(half):
             for offset in (-3, 3):
@@ -273,20 +272,17 @@
                     scatter1(half, way, step).start()
 
         near(0)
-        product(0, 0, first=True)
         near(1)
-        product(0, 1, -1)
-        product(0, 2, -2)
-        product(1, 0, first=True)
+        product((0, 1), 0, first=True)
+        product((0, 1), 1, -1)
         distant(0)
-        product(1, 1, -1)
-        product(0, 3, -3)
-        product(0, 4, last=True)
+        product((0, 1), 2, -2)
+        product((0,), 3, -3)
+        product((0,), 4, last=True)
         scatter(0)
         distant(1)
-        product(1, 2, -2)
-        product(1, 3, -3)
-        product(1, 4, last=True)
+        product((1,), 3, -3)
+        product((1,), 4, last=True)
         scatter(1)
 
         for half in range(2):
@@ -324,9 +320,8 @@
         gram_send1[...] = own
         gram_got1[col] = own
 
-        @pl.loop(1, 16, unroll=5)
-        def _(step):
-            gram1(step).start()
+        for over in FAR_COL:
+            gram1(*over).start()
 
         for copy in sends:
             copy.wait_send()
@@ -341,9 +336,8 @@
         gram_send2[...] = own
         gram_got2[row] = own
 
-        @pl.loop(1, 16, unroll=5)
-        def _(step):
-            gram2(step).start()
+        for over in FAR_ROW:
+            gram2(*over).start()
 
         all_waits(gram_got2.at[pl.ds(0, 15)], gram_sem.at[3])
 
@@ -383,7 +377,7 @@
     tile_cols,
     tile_count,
 ):
-    dense = build_dense(tile_rows, tile_cols, tile_count[0], tile_values[0, 0])
+    dense = build_dense((tile_cols * 16 + tile_rows)[0, 0], tile_count[0], tile_values[0, 0])
     dma = pltpu.SemaphoreType.DMA
     vmem = pl.BlockSpec(memory_space=pltpu.VMEM)
     hbm = pl.BlockSpec(memory_space=pl.ANY)

time: 129 us -> 124 us (0.961)
  Pallas kernels: 124 us -> 121 us
  local copies, waits for them, and re-layouts: 2.69 us -> 1.34 us
    pallas_call x1, Pallas kernels: 120 us -> 116 us  [on_device(): pl.pallas_call(main_kernel, out_shape=(block, block), in_specs=[vmem] * 4...]
    unnamed x18 -> x14, local copies, waits for them, and re-layouts: 2.69 us -> 1.34 us
where the time goes in v3:
time: 124 us
  Pallas kernels  121 us (98%)
  between operations  1.37 us (1%)
  local copies, waits for them, and re-layouts  1.34 us (1%)
    pallas_call x1, Pallas kernels, on_device(): pl.pallas_call(main_kernel, out_shape=(block, block), in_specs=[vmem] * 4...  116 us
    pallas_call x1, Pallas kernels, build_dense(): pl.pallas_call(build_kernel, out_shape=jax.ShapeDtypeStruct((256, TILE, T...  4.94 us

profile of v3, /device:TPU:1, one launch (start us, length us, event | category | flops | bytes accessed | tf_op | source)
XLA Modules:
  0.0 124.3 jit_solution(2524189438152007756)
XLA Ops:
  1.3 0.7 multiply_add_fusion
  2.0 0.0 copy-start
  2.0 0.0 copy-start.1
  2.0 0.0 copy-start.2
  2.0 0.0 copy-start.3
  2.0 0.0 copy-start.4
  2.0 0.0 copy-start.5
  2.0 4.9 %build_dense.1.dense = bf16[256,128,128]{2,1,0:T(8,128)(2,1)S(1)} custom-call(s32[256]{0:T(256)S(1)} %bitcast.4, s32[1]{0:T(128)} %bitcast.3.count_ref, bf16[256,128,128]{2,1,0:T(8,128)(2,1)} %bitcast.5), custom_call_target="tpu_custom_call" | custom-call | tf_op jit(solution)/shard_map/build_dense/pallas_call | solution.py:46
  7.0 0.0 copy-done
  7.0 0.0 copy-done.1
  7.0 0.0 copy-done.2
  7.0 0.0 copy-done.3
  7.0 0.0 copy-done.4
  7.0 0.0 copy-done.5
  7.0 115.9 %anderson.1 = (f32[128,256]{1,0:T(8,128)S(1)}, f32[128,256]{1,0:T(8,128)S(1)}) custom-call(f32[128,256]{1,0:T(8,128)S(1)} %copy-done.2, bf16[128,128]{1,0:T(8,128)(2,1)S(1)} %copy-done.5, bf16[128,256]{1,0:T(8,128)(2,1)S(1)} %copy-done.4, bf16[256,256]{1,0:T(8,128)(2,1)S(1)} %copy-done.3, f32[5,128,256]{2,1,0:T(8,128)S(1)} %copy-done, ...), custom_call_target="tpu_custom_call" | custom-call | tf_op jit(solution)/shard_map/anderson/pallas_call | solution.py:388
  123.0 0.7 copy.15
  123.6 0.7 copy.16
Async XLA Ops:
  2.0 5.0 %copy-start = (f32[5,128,256]{2,1,0:T(8,128)S(1)}, f32[5,128,256]{2,1,0:T(8,128)}, u32[]{:S(2)}) copy-start(f32[5,128,256]{2,1,0:T(8,128)} %past_images_ref.1) | copy-start | bytes 1966084
  2.0 5.0 %copy-start.1 = (f32[5,128,256]{2,1,0:T(8,128)S(1)}, f32[5,128,256]{2,1,0:T(8,128)}, u32[]{:S(2)}) copy-start(f32[5,128,256]{2,1,0:T(8,128)} %past_residuals_ref.1) | copy-start | bytes 1966084
  2.0 5.0 %copy-start.2 = (f32[128,256]{1,0:T(8,128)S(1)}, f32[128,256]{1,0:T(8,128)}, u32[]{:S(2)}) copy-start(f32[128,256]{1,0:T(8,128)} %iterate_ref.1) | copy-start | bytes 393220
  2.0 5.0 %copy-start.3 = (bf16[256,256]{1,0:T(8,128)(2,1)S(1)}, bf16[256,256]{1,0:T(8,128)(2,1)}, u32[]{:S(2)}) copy-start(bf16[256,256]{1,0:T(8,128)(2,1)} %mix_weight_ref.1) | copy-start | bytes 393220
  2.0 5.0 %copy-start.4 = (bf16[128,256]{1,0:T(8,128)(2,1)S(1)}, bf16[128,256]{1,0:T(8,128)(2,1)}, u32[]{:S(2)}) copy-start(bf16[128,256]{1,0:T(8,128)(2,1)} %input_weight_ref.1) | copy-start | bytes 196612
  2.0 5.0 %copy-start.5 = (bf16[128,128]{1,0:T(8,128)(2,1)S(1)}, bf16[128,128]{1,0:T(8,128)(2,1)}, u32[]{:S(2)}) copy-start(bf16[128,128]{1,0:T(8,128)(2,1)} %features_ref.1) | copy-start | bytes 98308

commit v4 on v3

--- a/solution.py
+++ b/solution.py
@@ -119,19 +119,19 @@
     first_axis, second_axis = (x, y), (y, x)
     sibling = row + 1 - 2 * core
 
+    barrier = pltpu.get_barrier_semaphore()
+    for (over_y, over_x), (over_z, over_core) in zip(FAR_COL, FAR_ROW):
+        to_col = 4 * lax.rem(y + over_y, 4) + lax.rem(x + over_x, 4)
+        to_row = 2 * lax.rem(z + over_z, 8) + lax.rem(core + over_core, 2)
+        pl.semaphore_signal(barrier, inc=1, device_id=(row, to_col), device_id_type=MESH)
+        pl.semaphore_signal(barrier, inc=1, device_id=(to_row, col), device_id_type=MESH)
+
     loads = []
     for half in range(2):
         for past_ref, kept in ((past_images_ref, images), (past_residuals_ref, residuals)):
             source = past_ref.at[pl.ds(1, 4), :, pl.ds(half * TILE, TILE)]
             loads.append(pltpu.make_async_copy(source, kept.at[pl.ds(0, 4), half], load_sem.at[len(loads)]))
             loads[-1].start()
-
-    barrier = pltpu.get_barrier_semaphore()
-
-    @pl.loop(1, 16)
-    def _(step):
-        pl.semaphore_signal(barrier, inc=1, device_id=(row, lax.rem(col + step, 16)), device_id_type=MESH)
-        pl.semaphore_signal(barrier, inc=1, device_id=(lax.rem(row + step, 16), col), device_id_type=MESH)
 
     state[...] = iterate_ref[...]
     inject[...] = jnp.dot(features_ref[...], input_weight_ref[...], preferred_element_type=F32)
@@ -216,7 +216,7 @@
 
     @pl.loop(0, ITERS)
     def _(k):
-        message = jnp.dot(state[...].astype(BF16), mix_weight_ref[...], preferred_element_type=F32).astype(BF16)
+        lowered = state[...].astype(BF16)
         sends = []
         used = [0, 0]
 
@@ -227,8 +227,12 @@
             used[half] += 1
 
         for half in range(2):
-            panel[half, row] = message[:, half * TILE : (half + 1) * TILE]
-            for offset in (2, -2, 0, 1, -1):
+            weight = mix_weight_ref[:, half * TILE : (half + 1) * TILE]
+            panel[half, row] = jnp.dot(lowered, weight, preferred_element_type=F32).astype(BF16)
+            for offset in (2, -2):
+                send(half, row, own_tile(offset))
+        for half in range(2):
+            for offset in (1, -1, 0):
                 send(half, row, sibling if offset == 0 else own_tile(offset))
 
         @pl.when(k == 0)
@@ -241,13 +245,15 @@
 
         low, high = pl.ds(0, TILE // 2), pl.ds(TILE // 2, TILE // 2)
 
-        def near(half):
+        def relay(half):
             for sign, part, extra in ((-1, low, None), (1, high, 16)):
                 tile = own_tile(2 * sign)
                 gather_wait(half, tile)
                 send(half, tile, own_tile(-2 * sign), part, tile if extra is None else extra)
                 send(half, tile, own_tile(-sign))
                 send(half, tile, sibling)
+
+        def adjacent(half):
             for sign in (-1, 1):
                 gather_wait(half, own_tile(sign))
                 send(half, own_tile(sign), sibling)
@@ -271,16 +277,18 @@
                 for way in range(2):
                     scatter1(half, way, step).start()
 
-        near(0)
-        near(1)
+        relay(0)
+        relay(1)
+        adjacent(0)
+        adjacent(1)
         product((0, 1), 0, first=True)
         product((0, 1), 1, -1)
         distant(0)
+        distant(1)
         product((0, 1), 2, -2)
         product((0,), 3, -3)
         product((0,), 4, last=True)
         scatter(0)
-        distant(1)
         product((1,), 3, -3)
         product((1,), 4, last=True)
         scatter(1)

time: 124 us -> 124 us (level)
  no operation moved by 1% of the time
where the time goes in v4:
time: 124 us
  Pallas kernels  121 us (98%)
  between operations  1.37 us (1%)
  local copies, waits for them, and re-layouts  1.34 us (1%)
    pallas_call x1, Pallas kernels, on_device(): pl.pallas_call(main_kernel, out_shape=(block, block), in_specs=[vmem] * 4...  116 us
    pallas_call x1, Pallas kernels, build_dense(): pl.pallas_call(build_kernel, out_shape=jax.ShapeDtypeStruct((256, TILE, T...  4.94 us

profile of v4, /device:TPU:1, one launch (start us, length us, event | category | flops | bytes accessed | tf_op | source)
XLA Modules:
  0.0 123.9 jit_solution(3826729322761354781)
XLA Ops:
  1.3 0.7 multiply_add_fusion
  2.0 0.0 copy-start
  2.0 0.0 copy-start.1
  2.0 0.0 copy-start.2
  2.0 0.0 copy-start.3
  2.0 0.0 copy-start.4
  2.0 0.0 copy-start.5
  2.0 4.9 %build_dense.1.dense = bf16[256,128,128]{2,1,0:T(8,128)(2,1)S(1)} custom-call(s32[256]{0:T(256)S(1)} %bitcast.4, s32[1]{0:T(128)} %bitcast.3.count_ref, bf16[256,128,128]{2,1,0:T(8,128)(2,1)} %bitcast.5), custom_call_target="tpu_custom_call" | custom-call | tf_op jit(solution)/shard_map/build_dense/pallas_call | solution.py:46
  7.0 0.0 copy-done
  7.0 0.0 copy-done.1
  7.0 0.0 copy-done.2
  7.0 0.0 copy-done.3
  7.0 0.0 copy-done.4
  7.0 0.0 copy-done.5
  7.0 115.6 %anderson.1 = (f32[128,256]{1,0:T(8,128)S(1)}, f32[128,256]{1,0:T(8,128)S(1)}) custom-call(f32[128,256]{1,0:T(8,128)S(1)} %copy-done.2, bf16[128,128]{1,0:T(8,128)(2,1)S(1)} %copy-done.5, bf16[128,256]{1,0:T(8,128)(2,1)S(1)} %copy-done.4, bf16[256,256]{1,0:T(8,128)(2,1)S(1)} %copy-done.3, f32[5,128,256]{2,1,0:T(8,128)S(1)} %copy-done, ...), custom_call_target="tpu_custom_call" | custom-call | tf_op jit(solution)/shard_map/anderson/pallas_call | solution.py:396
  122.6 0.7 copy.15
  123.3 0.7 copy.16
Async XLA Ops:
  2.0 5.0 %copy-start = (f32[5,128,256]{2,1,0:T(8,128)S(1)}, f32[5,128,256]{2,1,0:T(8,128)}, u32[]{:S(2)}) copy-start(f32[5,128,256]{2,1,0:T(8,128)} %past_images_ref.1) | copy-start | bytes 1966084
  2.0 5.0 %copy-start.1 = (f32[5,128,256]{2,1,0:T(8,128)S(1)}, f32[5,128,256]{2,1,0:T(8,128)}, u32[]{:S(2)}) copy-start(f32[5,128,256]{2,1,0:T(8,128)} %past_residuals_ref.1) | copy-start | bytes 1966084
  2.0 5.0 %copy-start.2 = (f32[128,256]{1,0:T(8,128)S(1)}, f32[128,256]{1,0:T(8,128)}, u32[]{:S(2)}) copy-start(f32[128,256]{1,0:T(8,128)} %iterate_ref.1) | copy-start | bytes 393220
  2.0 5.0 %copy-start.3 = (bf16[256,256]{1,0:T(8,128)(2,1)S(1)}, bf16[256,256]{1,0:T(8,128)(2,1)}, u32[]{:S(2)}) copy-start(bf16[256,256]{1,0:T(8,128)(2,1)} %mix_weight_ref.1) | copy-start | bytes 393220
  2.0 5.0 %copy-start.4 = (bf16[128,256]{1,0:T(8,128)(2,1)S(1)}, bf16[128,256]{1,0:T(8,128)(2,1)}, u32[]{:S(2)}) copy-start(bf16[128,256]{1,0:T(8,128)(2,1)} %input_weight_ref.1) | copy-start | bytes 196612
  2.0 5.0 %copy-start.5 = (bf16[128,128]{1,0:T(8,128)(2,1)S(1)}, bf16[128,128]{1,0:T(8,128)(2,1)}, u32[]{:S(2)}) copy-start(bf16[128,128]{1,0:T(8,128)(2,1)} %features_ref.1) | copy-start | bytes 98308

commit v5 on v4

--- a/solution.py
+++ b/solution.py
@@ -235,6 +235,11 @@
             for offset in (1, -1, 0):
                 send(half, row, sibling if offset == 0 else own_tile(offset))
 
+        @pl.when(k > 0)
+        def _():
+            all_waits(gram_got1.at[pl.ds(0, 15)], gram_sem.at[0])
+            all_waits(gram_got2.at[pl.ds(0, 15)], gram_sem.at[2])
+
         @pl.when(k == 0)
         def _():
             for load in loads:
@@ -365,9 +370,8 @@
                 mixed += alpha[pos] * images[k + pos, half]
             state[:, half * TILE : (half + 1) * TILE] = mixed
 
-        all_waits(gram_got1.at[pl.ds(0, 15)], gram_sem.at[0])
-        all_waits(gram_got2.at[pl.ds(0, 15)], gram_sem.at[2])
-
+    all_waits(gram_got1.at[pl.ds(0, 15)], gram_sem.at[0])
+    all_waits(gram_got2.at[pl.ds(0, 15)], gram_sem.at[2])
     state_out[...] = state[...]
     for half in range(2):
         residual_out[:, half * TILE : (half + 1) * TILE] = residuals[ITERS + 3, half]

time: 124 us -> 124 us (level)
  no operation moved by 1% of the time
where the time goes in v5:
time: 124 us
  Pallas kernels  121 us (98%)
  between operations  1.37 us (1%)
  local copies, waits for them, and re-layouts  1.34 us (1%)
    pallas_call x1, Pallas kernels, on_device(): pl.pallas_call(main_kernel, out_shape=(block, block), in_specs=[vmem] * 4...  116 us
    pallas_call x1, Pallas kernels, build_dense(): pl.pallas_call(build_kernel, out_shape=jax.ShapeDtypeStruct((256, TILE, T...  4.94 us

profile of v5, /device:TPU:1, one launch (start us, length us, event | category | flops | bytes accessed | tf_op | source)
XLA Modules:
  0.0 123.9 jit_solution(2575307036334082404)
XLA Ops:
  1.3 0.7 multiply_add_fusion
  2.0 0.0 copy-start
  2.0 0.0 copy-start.1
  2.0 0.0 copy-start.2
  2.0 0.0 copy-start.3
  2.0 0.0 copy-start.4
  2.0 0.0 copy-start.5
  2.0 4.9 %build_dense.1.dense = bf16[256,128,128]{2,1,0:T(8,128)(2,1)S(1)} custom-call(s32[256]{0:T(256)S(1)} %bitcast.4, s32[1]{0:T(128)} %bitcast.3.count_ref, bf16[256,128,128]{2,1,0:T(8,128)(2,1)} %bitcast.5), custom_call_target="tpu_custom_call" | custom-call | tf_op jit(solution)/shard_map/build_dense/pallas_call | solution.py:46
  7.0 0.0 copy-done
  7.0 0.0 copy-done.1
  7.0 0.0 copy-done.2
  7.0 0.0 copy-done.3
  7.0 0.0 copy-done.4
  7.0 0.0 copy-done.5
  7.0 115.6 %anderson.1 = (f32[128,256]{1,0:T(8,128)S(1)}, f32[128,256]{1,0:T(8,128)S(1)}) custom-call(f32[128,256]{1,0:T(8,128)S(1)} %copy-done.2, bf16[128,128]{1,0:T(8,128)(2,1)S(1)} %copy-done.5, bf16[128,256]{1,0:T(8,128)(2,1)S(1)} %copy-done.4, bf16[256,256]{1,0:T(8,128)(2,1)S(1)} %copy-done.3, f32[5,128,256]{2,1,0:T(8,128)S(1)} %copy-done, ...), custom_call_target="tpu_custom_call" | custom-call | tf_op jit(solution)/shard_map/anderson/pallas_call | solution.py:400
  122.6 0.7 copy.15
  123.3 0.7 copy.16
Async XLA Ops:
  2.0 5.0 %copy-start = (f32[5,128,256]{2,1,0:T(8,128)S(1)}, f32[5,128,256]{2,1,0:T(8,128)}, u32[]{:S(2)}) copy-start(f32[5,128,256]{2,1,0:T(8,128)} %past_images_ref.1) | copy-start | bytes 1966084
  2.0 5.0 %copy-start.1 = (f32[5,128,256]{2,1,0:T(8,128)S(1)}, f32[5,128,256]{2,1,0:T(8,128)}, u32[]{:S(2)}) copy-start(f32[5,128,256]{2,1,0:T(8,128)} %past_residuals_ref.1) | copy-start | bytes 1966084
  2.0 5.0 %copy-start.2 = (f32[128,256]{1,0:T(8,128)S(1)}, f32[128,256]{1,0:T(8,128)}, u32[]{:S(2)}) copy-start(f32[128,256]{1,0:T(8,128)} %iterate_ref.1) | copy-start | bytes 393220
  2.0 5.0 %copy-start.3 = (bf16[256,256]{1,0:T(8,128)(2,1)S(1)}, bf16[256,256]{1,0:T(8,128)(2,1)}, u32[]{:S(2)}) copy-start(bf16[256,256]{1,0:T(8,128)(2,1)} %mix_weight_ref.1) | copy-start | bytes 393220
  2.0 5.0 %copy-start.4 = (bf16[128,256]{1,0:T(8,128)(2,1)S(1)}, bf16[128,256]{1,0:T(8,128)(2,1)}, u32[]{:S(2)}) copy-start(bf16[128,256]{1,0:T(8,128)(2,1)} %input_weight_ref.1) | copy-start | bytes 196612
  2.0 5.0 %copy-start.5 = (bf16[128,128]{1,0:T(8,128)(2,1)S(1)}, bf16[128,128]{1,0:T(8,128)(2,1)}, u32[]{:S(2)}) copy-start(bf16[128,128]{1,0:T(8,128)(2,1)} %features_ref.1) | copy-start | bytes 98308
